TPU v7x, 128 devices: a whole 4x4x4 slice. The times are simulated.
128 devices in a mesh: dp: 32 (over y, x, z_lo), tensor: 4 (over z_hi, core).
Axes of the slice: x: 4, y: 4, z: 4 (z_hi: 2, z_lo: 2; z = z_hi * 2 + z_lo), core: 2. Of those that a mesh axis runs over, the one named last changes fastest.
Arguments:
- tokens: bfloat16 [16384, 1024], P(('dp', 'tensor')), may hold values from -6 to 6
- cotangent: bfloat16 [16384, 1024], P(('dp', 'tensor')), may hold values from -6 to 6
- norm1_gain: bfloat16 [1024], P('dp'), may hold values from 0.25 to 1.75
- w_query: bfloat16 [1024, 1024], P('dp', 'tensor'), may hold values from -0.1875 to 0.1875
- w_key: bfloat16 [1024, 512], P('dp', 'tensor'), may hold values from -0.1875 to 0.1875
- w_value: bfloat16 [1024, 512], P('dp', 'tensor'), may hold values from -0.1875 to 0.1875
- w_out: bfloat16 [1024, 1024], P('dp', 'tensor'), may hold values from -0.75 to 0.75
- norm2_gain: bfloat16 [1024], P('dp'), may hold values from 0.25 to 1.75
- expert_gate: bfloat16 [32, 1024, 512], P('dp', None, 'tensor'), may hold values from -0.1875 to 0.1875
- expert_up: bfloat16 [32, 1024, 512], P('dp', None, 'tensor'), may hold values from -0.1875 to 0.1875
- expert_down: bfloat16 [32, 512, 1024], P('dp', 'tensor'), may hold values from -0.25 to 0.25
- route_gates: float32 [16384, 8], P('dp'), may hold values from 0.15 to 0.6
- routes: int32 [16384, 8], P('dp'), may hold values from 0 to 31, all different within a row; in each aligned block of 512 rows (0 to 511, 512 to 1023, ...) at most 160 rows name the same one
- segment: int32 [16384], P('dp'), may hold values from 0 to 2, as said below
Outputs:
- output: float32 [16384, 1024], P(('dp', 'tensor'))
- grad_tokens: float32 [16384, 1024], P(('dp', 'tensor'))
- grad_norm1_gain: float32 [1024], P(('dp', 'tensor'))
- grad_w_query: float32 [1024, 1024], P('dp', 'tensor')
- grad_w_key: float32 [1024, 512], P('dp', 'tensor')
- grad_w_value: float32 [1024, 512], P('dp', 'tensor')
- grad_w_out: float32 [1024, 1024], P('dp', 'tensor')
- grad_norm2_gain: float32 [1024], P(('dp', 'tensor'))
- grad_expert_gate: float32 [32, 1024, 512], P('dp', None, 'tensor')
- grad_expert_up: float32 [32, 1024, 512], P('dp', None, 'tensor')
- grad_expert_down: float32 [32, 512, 1024], P('dp', 'tensor')
Inputs may be any that keep to these rules, and one draw needn't show every extreme that they name: `segment`: each group of 512 rows holds 3 documents numbered 0, 1, 2 in order; the first and the last hold 1 to 64 rows each. `routes`: the 8 experts of a row are distinct; within each group of 512 rows no expert is named by more than 160 rows, and one is named by exactly 160.
All inputs are finite; a program needn't handle non-finite values.
Results may differ from a plain program's by a relative error of at most 0.035.
Values may be sent and summed in bfloat16 or wider, within the bound.
No kernel may reach another device: no remote copies, remote signals or barrier semaphores. Data moves between devices by JAX's collectives and lax.ppermute only.
A program may use at most 192 MiB of HBM per device.

v0:
```python
import jax
import jax.numpy as jnp
from jax import lax
from jax.sharding import PartitionSpec as P

HD = 64
DOCS = 3


EPS = 1e-06
THETA = 10000.0


def rms_forward(rows, gain):
    inverse = lax.rsqrt(jnp.mean(rows * rows, axis=1, keepdims=True) + EPS)
    normal = rows * inverse
    return (normal, inverse, normal * gain[None, :])


def rms_backward(grad_out, normal, inverse, gain):
    scaled = grad_out * gain[None, :]
    inner = jnp.mean(scaled * normal, axis=1, keepdims=True)
    return (inverse * (scaled - normal * inner), jnp.sum(grad_out * normal, axis=0))


def doc_positions(segment):
    onehot = (segment[:, None] == jnp.arange(DOCS, dtype=jnp.int32)[None, :]).astype(jnp.int32)
    counts = jnp.sum(onehot, axis=0)
    starts = jnp.cumsum(counts) - counts
    first = jnp.sum(onehot * starts[None, :], axis=1)
    return jnp.arange(segment.shape[0], dtype=jnp.int32) - first


def rope_tables(segment, size):
    places = doc_positions(segment).astype(jnp.float32)
    freqs = THETA ** (-(jnp.arange(size // 2, dtype=jnp.float32) * 2.0) / size)
    angle = places[:, None] * freqs[None, :]
    return (jnp.cos(angle), jnp.sin(angle))


def rotate(values, cosine, sine, heads):
    split = values.reshape(values.shape[0], heads, 2, -1)
    first = split[:, :, 0]
    second = split[:, :, 1]
    cos_b = cosine[:, None, :]
    sin_b = sine[:, None, :]
    turned = jnp.stack([first * cos_b - second * sin_b, second * cos_b + first * sin_b], axis=2)
    return turned.reshape(values.shape)


def block_scores(qpart, keys, start, segment):
    rows = qpart.shape[0]
    scores = jnp.einsum(
        "qkrd,skd->krqs", qpart, keys, preferred_element_type=jnp.float32
    ) * qpart.shape[-1] ** (-0.5)
    qidx = start + jnp.arange(rows, dtype=jnp.int32)
    kidx = jnp.arange(segment.shape[0], dtype=jnp.int32)
    allowed = (segment[:, None] == segment[None, :]) & (kidx[None, :] <= qidx[:, None])
    return jnp.where(allowed[None, None], scores, -1e30)


def attend(queries, keys, values, segment, block):
    count = queries.shape[0]
    starts = jnp.arange(count // block, dtype=jnp.int32) * block

    def one_block(start):
        scores = block_scores(queries, keys, start, segment)
        top = jnp.max(scores, axis=3, keepdims=True)
        weights = jnp.exp(scores - top)
        total = jnp.sum(weights, axis=3, keepdims=True)
        probs = (weights / total).astype(jnp.bfloat16)
        out = jnp.einsum("krqs,skd->qkrd", probs, values, preferred_element_type=jnp.float32)
        return (out, top + jnp.log(total))

    outs, logsum = lax.map(one_block, starts)
    return (outs.reshape(count, -1), logsum)


def attend_back(queries, keys, values, segment, logsum, grad_out, block):
    count = queries.shape[0]
    starts = jnp.arange(count // block, dtype=jnp.int32) * block
    scale = queries.shape[-1] ** (-0.5)

    def one_block(carry, item):
        start, lse = item
        scores = block_scores(queries, keys, start, segment)
        probs = jnp.exp(scores - lse)
        grad_probs = jnp.einsum(
            "qkrd,skd->krqs", grad_out, values, preferred_element_type=jnp.float32
        )
        inner = jnp.sum(probs * grad_probs, axis=3, keepdims=True)
        grad_scores = (probs * (grad_probs - inner)).astype(jnp.bfloat16)
        grad_q = (
            jnp.einsum("krqs,skd->qkrd", grad_scores, keys, preferred_element_type=jnp.float32)
            * scale
        )
        grad_k = (
            carry[0]
            + jnp.einsum("krqs,qkrd->skd", grad_scores, queries, preferred_element_type=jnp.float32)
            * scale
        )
        grad_v = carry[1] + jnp.einsum(
            "krqs,qkrd->skd",
            probs.astype(jnp.bfloat16),
            grad_out,
            preferred_element_type=jnp.float32,
        )
        return ((grad_k, grad_v), grad_q)

    zeros = jnp.zeros(keys.shape, jnp.float32)
    (grad_k, grad_v), grad_q = lax.scan(one_block, (zeros, zeros), (starts, logsum))
    return (grad_q.reshape(count, -1), grad_k.reshape(count, -1), grad_v.reshape(count, -1))


def expert_front(inputs, expert_gate, expert_up):
    gate_pre = jnp.einsum("sjcd,jdf->sjcf", inputs, expert_gate, preferred_element_type=jnp.float32)
    up_pre = jnp.einsum("sjcd,jdf->sjcf", inputs, expert_up, preferred_element_type=jnp.float32)
    hidden = (jax.nn.silu(gate_pre) * up_pre).astype(jnp.bfloat16)
    return (gate_pre, up_pre, hidden)


def send_slots(slots):
    return lax.all_to_all(slots, "dp", split_axis=0, concat_axis=0, tiled=True)


def return_slots(slots):
    return lax.all_to_all(slots, "dp", split_axis=0, concat_axis=0, tiled=True)


def on_device(
    tokens,
    cotangent,
    norm1_gain,
    w_query,
    w_key,
    w_value,
    w_out,
    norm2_gain,
    expert_gate,
    expert_up,
    expert_down,
    route_gates,
    routes,
    segment,
):
    group = segment.shape[0]
    local = tokens.shape[0]
    width = tokens.shape[1]
    top_k = routes.shape[1]
    dp_count = lax.axis_size("dp")
    tensor_count = lax.axis_size("tensor")
    experts = expert_gate.shape[0] * dp_count
    capacity = min(group, group * top_k * 5 // (4 * experts)) // tensor_count * tensor_count
    block = min(512, group)
    q_local = w_query.shape[1] // HD
    kv_local = w_key.shape[1] // HD
    ratio = q_local // kv_local
    here = lax.axis_index("tensor")
    wq, wk, wv, wo, gain1, gain2 = (
        lax.all_gather(w_query, "dp", axis=0, tiled=True),
        lax.all_gather(w_key, "dp", axis=0, tiled=True),
        lax.all_gather(w_value, "dp", axis=0, tiled=True),
        lax.all_gather(w_out, "dp", axis=0, tiled=True),
        lax.all_gather(norm1_gain, "dp", axis=0, tiled=True),
        lax.all_gather(norm2_gain, "dp", axis=0, tiled=True),
    )
    gain1 = gain1.astype(jnp.float32)
    gain2 = gain2.astype(jnp.float32)
    rows = lax.all_gather(tokens, "tensor", axis=0, tiled=True).astype(jnp.float32)
    normal1, inverse1, scaled1 = rms_forward(rows, gain1)
    normed1 = scaled1.astype(jnp.bfloat16)
    cosine, sine = rope_tables(segment, HD)
    queries = rotate(
        jnp.dot(normed1, wq, preferred_element_type=jnp.float32), cosine, sine, q_local
    )
    queries = queries.astype(jnp.bfloat16).reshape(group, kv_local, ratio, HD)
    keys = rotate(jnp.dot(normed1, wk, preferred_element_type=jnp.float32), cosine, sine, kv_local)
    keys = keys.astype(jnp.bfloat16).reshape(group, kv_local, HD)
    values = (
        jnp.dot(normed1, wv, preferred_element_type=jnp.float32)
        .astype(jnp.bfloat16)
        .reshape(group, kv_local, HD)
    )
    attended, logsum = attend(queries, keys, values, segment, block)
    attended = attended.astype(jnp.bfloat16)
    partial_value = jnp.einsum("gh,dh->gd", attended, wo, preferred_element_type=jnp.float32)
    mixed = rows + lax.psum(partial_value, "tensor")
    normal2, inverse2, scaled2 = rms_forward(mixed, gain2)
    normed2 = scaled2.astype(jnp.bfloat16)
    flat = routes.reshape(-1)
    onehot = (flat[:, None] == jnp.arange(experts, dtype=jnp.int32)[None, :]).astype(jnp.int32)
    slot = jnp.sum((jnp.cumsum(onehot, axis=0) - 1) * onehot, axis=1)
    dest = flat * capacity + slot
    empty = jnp.zeros((experts * capacity, width), jnp.bfloat16)
    packed = (
        empty.at[dest].set(jnp.repeat(normed2, top_k, axis=0)).reshape(experts, capacity, width)
    )
    arrived = send_slots(packed)
    arrived = arrived.reshape(dp_count, expert_gate.shape[0], capacity, width)
    gate_pre, up_pre, hidden = expert_front(arrived, expert_gate, expert_up)
    produced = jnp.einsum(
        "sjcf,jfd->sjcd", hidden, expert_down, preferred_element_type=jnp.float32
    ).astype(jnp.bfloat16)
    returned = return_slots(produced.reshape(experts, capacity, width))
    picked = returned.reshape(experts * capacity, width)[dest].reshape(group, top_k, width)
    moe_part = jnp.sum(picked * route_gates[:, :, None], axis=1)
    moe = lax.psum_scatter(
        moe_part.astype(jnp.bfloat16), "tensor", scatter_dimension=0, tiled=True
    ).astype(jnp.float32)
    output = lax.dynamic_slice_in_dim(mixed, here * local, local, 0) + moe
    grad_rows = lax.all_gather(cotangent, "tensor", axis=0, tiled=True).astype(jnp.float32)
    grad_slots = (
        (grad_rows[:, None, :] * route_gates[:, :, None]).reshape(-1, width).astype(jnp.bfloat16)
    )
    grad_packed = empty.at[dest].set(grad_slots).reshape(experts, capacity, width)
    grad_arrived = send_slots(grad_packed).reshape(arrived.shape)
    inputs = send_slots(packed).reshape(arrived.shape)
    gate_pre, up_pre, hidden = expert_front(inputs, expert_gate, expert_up)
    sigma = jax.nn.sigmoid(gate_pre)
    grad_down = jnp.einsum(
        "sjcf,sjcd->jfd", hidden, grad_arrived, preferred_element_type=jnp.float32
    )
    grad_hidden = jnp.einsum(
        "sjcd,jfd->sjcf", grad_arrived, expert_down, preferred_element_type=jnp.float32
    )
    grad_gate_pre = (grad_hidden * up_pre * sigma * (1.0 + gate_pre * (1.0 - sigma))).astype(
        jnp.bfloat16
    )
    grad_up_pre = (grad_hidden * gate_pre * sigma).astype(jnp.bfloat16)
    grad_gate = jnp.einsum(
        "sjcd,sjcf->jdf", inputs, grad_gate_pre, preferred_element_type=jnp.float32
    )
    grad_up = jnp.einsum("sjcd,sjcf->jdf", inputs, grad_up_pre, preferred_element_type=jnp.float32)
    grad_inputs = jnp.einsum(
        "sjcf,jdf->sjcd", grad_gate_pre, expert_gate, preferred_element_type=jnp.float32
    )
    grad_inputs = (
        grad_inputs
        + jnp.einsum("sjcf,jdf->sjcd", grad_up_pre, expert_up, preferred_element_type=jnp.float32)
    ).astype(jnp.bfloat16)
    grad_back = return_slots(grad_inputs.reshape(experts, capacity, width))
    grad_picked = grad_back.reshape(experts * capacity, width)[dest].reshape(group, top_k, width)
    grad_normed2 = jnp.sum(grad_picked, axis=1, dtype=jnp.float32)
    grad_mixed_part, gain2_part = rms_backward(grad_normed2, normal2, inverse2, gain2)
    grad_mixed, gain2_full = lax.psum((grad_mixed_part, gain2_part), "tensor")
    grad_mixed = grad_mixed + grad_rows
    grad_branch = grad_mixed.astype(jnp.bfloat16)
    grad_wo = jnp.einsum("gd,gh->dh", grad_branch, attended, preferred_element_type=jnp.float32)
    grad_attended = jnp.dot(grad_branch, wo, preferred_element_type=jnp.float32).astype(
        jnp.bfloat16
    )
    grad_attended = grad_attended.reshape(group, kv_local, ratio, HD)
    grad_q, grad_k, grad_v = attend_back(
        queries, keys, values, segment, logsum, grad_attended, block
    )
    grad_q = rotate(grad_q, cosine, -sine, q_local).astype(jnp.bfloat16)
    grad_k = rotate(grad_k, cosine, -sine, kv_local).astype(jnp.bfloat16)
    grad_v = grad_v.astype(jnp.bfloat16)
    grad_wq = jnp.einsum("gd,gh->dh", normed1, grad_q, preferred_element_type=jnp.float32)
    grad_wk = jnp.einsum("gd,gh->dh", normed1, grad_k, preferred_element_type=jnp.float32)
    grad_wv = jnp.einsum("gd,gh->dh", normed1, grad_v, preferred_element_type=jnp.float32)
    grad_normed1 = jnp.einsum("gh,dh->gd", grad_q, wq, preferred_element_type=jnp.float32)
    grad_normed1 = grad_normed1 + jnp.einsum(
        "gh,dh->gd", grad_k, wk, preferred_element_type=jnp.float32
    )
    grad_normed1 = grad_normed1 + jnp.einsum(
        "gh,dh->gd", grad_v, wv, preferred_element_type=jnp.float32
    )
    grad_rows_part, gain1_part = rms_backward(grad_normed1, normal1, inverse1, gain1)
    gain1_order = gain1_part.reshape(dp_count, tensor_count, -1).transpose(1, 0, 2).reshape(-1)
    grad_own, gain1_share = (
        lax.psum_scatter(
            grad_rows_part.astype(jnp.bfloat16), "tensor", scatter_dimension=0, tiled=True
        ).astype(jnp.float32),
        lax.psum_scatter(
            gain1_order.astype(jnp.bfloat16), "tensor", scatter_dimension=0, tiled=True
        ).astype(jnp.float32),
    )
    grad_tokens = lax.dynamic_slice_in_dim(grad_mixed, here * local, local, 0) + grad_own
    grad_wq_s, grad_wk_s, grad_wv_s, grad_wo_s, gain1_grad, gain2_share = (
        lax.psum_scatter(
            grad_wq.astype(jnp.bfloat16), "dp", scatter_dimension=0, tiled=True
        ).astype(jnp.float32),
        lax.psum_scatter(
            grad_wk.astype(jnp.bfloat16), "dp", scatter_dimension=0, tiled=True
        ).astype(jnp.float32),
        lax.psum_scatter(
            grad_wv.astype(jnp.bfloat16), "dp", scatter_dimension=0, tiled=True
        ).astype(jnp.float32),
        lax.psum_scatter(
            grad_wo.astype(jnp.bfloat16), "dp", scatter_dimension=0, tiled=True
        ).astype(jnp.float32),
        lax.psum_scatter(
            gain1_share.astype(jnp.bfloat16), "dp", scatter_dimension=0, tiled=True
        ).astype(jnp.float32),
        lax.psum_scatter(
            gain2_full.astype(jnp.bfloat16), "dp", scatter_dimension=0, tiled=True
        ).astype(jnp.float32),
    )
    piece = width // (dp_count * tensor_count)
    gain2_grad = lax.dynamic_slice_in_dim(gain2_share, here * piece, piece, 0)
    return (
        output,
        grad_tokens,
        gain1_grad,
        grad_wq_s,
        grad_wk_s,
        grad_wv_s,
        grad_wo_s,
        gain2_grad,
        grad_gate,
        grad_up,
        grad_down,
    )


def solution(mesh):
    in_specs = (
        P(("dp", "tensor"), None),
        P(("dp", "tensor"), None),
        P("dp"),
        P("dp", "tensor"),
        P("dp", "tensor"),
        P("dp", "tensor"),
        P("dp", "tensor"),
        P("dp"),
        P("dp", None, "tensor"),
        P("dp", None, "tensor"),
        P("dp", "tensor", None),
        P("dp", None),
        P("dp", None),
        P("dp"),
    )
    out_specs = (
        P(("dp", "tensor"), None),
        P(("dp", "tensor"), None),
        P(("dp", "tensor")),
        P("dp", "tensor"),
        P("dp", "tensor"),
        P("dp", "tensor"),
        P("dp", "tensor"),
        P(("dp", "tensor")),
        P("dp", None, "tensor"),
        P("dp", None, "tensor"),
        P("dp", "tensor", None),
    )
    return jax.shard_map(
        on_device, mesh=mesh, in_specs=in_specs, out_specs=out_specs, check_vma=False
    )
```

profile of v0, /device:TPU:1, one launch (start us, length us, event | category | flops | bytes accessed | tf_op | source)
XLA Modules:
  0.0 1993.6 jit_solution(16746041713671480059)
XLA Ops:
  12.7 70.2 %all-reduce.6 = (bf16[1024]{0:T(1024)(128)(2,1)S(1)}, bf16[1024]{0:T(1024)(128)(2,1)S(1)}) all-reduce(bf16[1024]{0:T(1024)(128)(2,1)S(1)} %dynamic-update-slice, bf16[1024]{0:T(1024)(128)(2,1)S(1)} %dynamic-update-slice.1), channel_id=1, replica_groups=mesh['dp'=32,'tensor'=4] {'dp'}, use_global_device_ids=true, to_apply=%add | all-reduce | flops 2048 | bytes 8192
  83.6 63.0 %all_gather.27 = bf16[1024,128]{1,0:T(8,128)(2,1)S(1)} all-gather(bf16[32,128]{1,0:T(8,128)(2,1)} %param.18), channel_id=1, replica_groups=mesh['dp'=32,'tensor'=4] {'dp'}, dimensions={0}, use_global_device_ids=true | all-gather | bytes 270336 | tf_op jit(solution)/shard_map/all_gather | solution.py:161
  146.6 64.8 %all_gather.26 = bf16[1024,128]{1,0:T(8,128)(2,1)S(1)} all-gather(bf16[32,128]{1,0:T(8,128)(2,1)} %param.19), channel_id=1, replica_groups=mesh['dp'=32,'tensor'=4] {'dp'}, dimensions={0}, use_global_device_ids=true | all-gather | bytes 270336 | tf_op jit(solution)/shard_map/all_gather | solution.py:162
  213.4 64.6 %all_gather.28 = bf16[1024,256]{1,0:T(8,128)(2,1)S(1)} all-gather(bf16[32,256]{1,0:T(8,128)(2,1)} %param.17), channel_id=1, replica_groups=mesh['dp'=32,'tensor'=4] {'dp'}, dimensions={0}, use_global_device_ids=true | all-gather | bytes 540672 | tf_op jit(solution)/shard_map/all_gather | solution.py:160
  278.1 65.9 %all_gather.29 = bf16[1024,256]{1,0:T(8,128)(2,1)S(1)} all-gather(bf16[32,256]{1,0:T(8,128)(2,1)} %param.20), channel_id=1, replica_groups=mesh['dp'=32,'tensor'=4] {'dp'}, dimensions={0}, use_global_device_ids=true | all-gather | bytes 540672 | tf_op jit(solution)/shard_map/all_gather | solution.py:163
  355.1 9.2 reduce-window.19
  366.5 114.0 %all-reduce.10.cloned.1.call-done = f32[512,1024]{1,0:T(8,128)} async-done(((f32[512,1024]{1,0:T(8,128)}), f32[512,1024]{1,0:T(8,128)}) %all-reduce.10.cloned.1.call-update) | async-done | bytes 2097168 | tf_op jit(solution)/shard_map/psum | solution.py:187
  480.5 1.9 multiply_reduce_fusion.2
  483.7 25.3 %scatter_custom_fusion = bf16[5120,1024]{1,0:T(8,128)(2,1)} fusion(s32[4096]{0:T(1024)} %bitcast.253, bf16[]{:T(256)} %constant.89.clone.1, bf16[512,1024]{1,0:T(8,128)(2,1)} %multiply_convert_fusion), kind=kCustom, calls=%fused_computation.11 | custom fusion | bytes 11534848 | tf_op jit(solution)/shard_map/scatter | solution.py:196
  509.0 7.0 all-to-all-start
  518.7 56.5 %all-gather.5.cloned.1.call-done = bf16[512,1024]{1,0:T(8,128)(2,1)} async-done(((bf16[128,1024]{1,0:T(8,128)(2,1)}), bf16[512,1024]{1,0:T(8,128)(2,1)}) %all-gather.5.cloned.1.call-update) | async-done | bytes 1048592 | tf_op jit(solution)/shard_map/all_gather | solution.py:211
  575.2 2.8 convert_element_type.207
  578.0 26.1 %scatter_custom_fusion.1 = bf16[5120,1024]{1,0:T(8,128)(2,1)} fusion(s32[4096]{0:T(1024)} %bitcast.254, f32[4096]{0:T(1024)S(1)} %mul.407, f32[512,1024]{1,0:T(8,128)} %convert_element_type.207, bf16[]{:T(256)} %constant.89.clone.1), kind=kCustom, calls=%fused_computation.10 | custom fusion | flops 8388608 | bytes 12599808 | tf_op jit(solution)/shard_map/scatter | solution.py:215
  604.1 71.8 %all-to-all-done = bf16[32,160,1024]{2,1,0:T(8,128)(2,1)} async-done(((bf16[32,160,1024]{2,1,0:T(8,128)(2,1)}), bf16[32,160,1024]{2,1,0:T(8,128)(2,1)}, u32[]{:S(2)}, u32[]{:S(2)}) %all-to-all-start) | async-done | bytes 10485792 | tf_op jit(solution)/shard_map/all_to_all | solution.py:123
  675.8 17.0 all-to-all-start.2
  692.8 8.4 fusion.78
  701.3 8.4 fusion.81
  709.7 140.2 %all-to-all-done.2 = bf16[32,160,1024]{2,1,0:T(8,128)(2,1)} async-done(((bf16[32,160,1024]{2,1,0:T(8,128)(2,1)}), bf16[32,160,1024]{2,1,0:T(8,128)(2,1)}, u32[]{:S(2)}, u32[]{:S(2)}) %all-to-all-start.2) | async-done | bytes 10485792 | tf_op jit(solution)/shard_map/all_to_all | solution.py:123
  849.9 10.7 fusion.24
  860.6 8.7 fusion.46
  869.3 14.2 add_convert_fusion
  883.5 18.7 all-to-all-start.3
  902.1 6.8 convolution_convert_fusion
  908.9 146.4 %all-to-all-done.3 = bf16[32,160,1024]{2,1,0:T(8,128)(2,1)} async-done(((bf16[32,160,1024]{2,1,0:T(8,128)(2,1)}), bf16[32,160,1024]{2,1,0:T(8,128)(2,1)}, u32[]{:S(2)}, u32[]{:S(2)}) %all-to-all-start.3) | async-done | bytes 10485792 | tf_op jit(solution)/shard_map/all_to_all | solution.py:127
  1055.3 23.6 %all-to-all-start.1 = ((bf16[32,160,1024]{2,1,0:T(8,128)(2,1)}), bf16[32,160,1024]{2,1,0:T(8,128)(2,1)}, u32[]{:S(2)}, u32[]{:S(2)}) async-start(bf16[32,160,1024]{2,1,0:T(8,128)(2,1)} %convolution_convert_fusion), calls=%async_computation.1 | async-start | bytes 20971520 | tf_op jit(solution)/shard_map/all_to_all | solution.py:127
  1079.0 26.6 %gather_fusion.1 = bf16[4096,1024]{1,0:T(8,128)(2,1)} fusion(bf16[5120,1024]{1,0:T(8,128)(2,1)} %bitcast.48, s32[4096]{0:T(1024)S(1)} %broadcast_clamp_fusion), kind=kCustom, calls=%fused_computation.1 | custom fusion | bytes 16793600 | tf_op jit(solution)/shard_map/gather | solution.py:242
  1105.6 11.9 convert_reduce_fusion
  1117.5 2.9 multiply_reduce_fusion
  1125.9 104.8 %all-to-all-done.1 = bf16[32,160,1024]{2,1,0:T(8,128)(2,1)} async-done(((bf16[32,160,1024]{2,1,0:T(8,128)(2,1)}), bf16[32,160,1024]{2,1,0:T(8,128)(2,1)}, u32[]{:S(2)}, u32[]{:S(2)}) %all-to-all-start.1) | async-done | bytes 10485792 | tf_op jit(solution)/shard_map/all_to_all | solution.py:127
  1230.8 26.5 %gather_fusion = bf16[4096,1024]{1,0:T(8,128)(2,1)} fusion(bf16[5120,1024]{1,0:T(8,128)(2,1)} %bitcast.35, s32[4096]{0:T(1024)S(1)} %broadcast_clamp_fusion), kind=kCustom, calls=%fused_computation | custom fusion | bytes 16793600 | tf_op jit(solution)/shard_map/gather | solution.py:205
  1257.3 9.6 fusion
  1267.0 2.3 convert_add_fusion.2
  1273.1 3.3 fusion.10
  1283.4 8.1 fusion.57
  1293.0 2.2 convolution_multiply_fusion
  1297.5 2.8 fusion.96
  1302.0 2.2 fusion.35
  1305.7 7.0 fusion.51
  1312.8 6.5 fusion.54
  1319.3 9.8 psum.23
  1329.3 7.2 all-reduce.2
  1336.5 75.6 %all-reduce.5 = (bf16[256]{0:T(256)(128)(2,1)S(1)}, bf16[1024]{0:T(1024)(128)(2,1)S(1)}) all-reduce(bf16[256]{0:T(256)(128)(2,1)S(1)} %dynamic-slice.4, bf16[1024]{0:T(1024)(128)(2,1)S(1)} %psum.23), channel_id=5, replica_groups=mesh['dp'=32,'tensor'=4] {'dp'}, use_global_device_ids=true, to_apply=%region_23.24.clone | all-reduce | flops 1280 | bytes 5120
  1415.2 38.0 %reduce-scatter.15.cloned.1.call-done = bf16[32,128]{1,0:T(8,128)(2,1)} async-done(((bf16[1024,128]{1,0:T(8,128)(2,1)}), bf16[32,128]{1,0:T(8,128)(2,1)}) %reduce-scatter.15.cloned.1.call-update) | async-done | bytes 8208 | tf_op jit(solution)/shard_map/reduce_scatter | solution.py:287
  1454.5 156.6 %reduce-scatter.13.cloned.1.call-done = bf16[32,128]{1,0:T(8,128)(2,1)} async-done(((bf16[1024,128]{1,0:T(8,128)(2,1)}), bf16[32,128]{1,0:T(8,128)(2,1)}) %reduce-scatter.13.cloned.1.call-update) | async-done | bytes 8208 | tf_op jit(solution)/shard_map/reduce_scatter | solution.py:284
  1612.5 156.5 %reduce-scatter.17.cloned.1.call-done = bf16[32,256]{1,0:T(8,128)(2,1)} async-done(((bf16[1024,256]{1,0:T(8,128)(2,1)}), bf16[32,256]{1,0:T(8,128)(2,1)}) %reduce-scatter.17.cloned.1.call-update) | async-done | bytes 16400 | tf_op jit(solution)/shard_map/reduce_scatter | solution.py:290
  1770.3 158.0 %reduce-scatter.11.cloned.1.call-done = bf16[32,256]{1,0:T(8,128)(2,1)} async-done(((bf16[1024,256]{1,0:T(8,128)(2,1)}), bf16[32,256]{1,0:T(8,128)(2,1)}) %reduce-scatter.11.cloned.1.call-update) | async-done | bytes 16400 | tf_op jit(solution)/shard_map/reduce_scatter | solution.py:281
  1929.7 54.8 %reduce-scatter.9.cloned.1.call-done = bf16[128,1024]{1,0:T(8,128)(2,1)} async-done(((bf16[512,1024]{1,0:T(8,128)(2,1)}), bf16[128,1024]{1,0:T(8,128)(2,1)}) %reduce-scatter.9.cloned.1.call-update) | async-done | bytes 262160 | tf_op jit(solution)/shard_map/reduce_scatter | solution.py:272
  1984.5 2.0 convert_add_fusion.1
  (203 shorter events, 54.2 us)
Async XLA Ops:
  7.2 842.7 %copy-start = (bf16[1,128,1024]{2,1,0:T(8,128)(2,1)S(1)}, bf16[1,128,1024]{2,1,0:T(8,128)(2,1)}, u32[]{:S(2)}) copy-start(bf16[1,128,1024]{2,1,0:T(8,128)(2,1)} %param.24) | copy-start | bytes 786436
  7.2 336.8 %all-gather.3.cloned.1.call-start = ((), (), s32[]{:S(2)}) async-start(), calls=%async_computation.10 | async-start | bytes 1310720 | tf_op jit(solution)/shard_map/all_gather | solution.py:169
  7.9 472.6 %all-reduce.10.cloned.1.call-start = ((), (), s32[]{:S(2)}) async-start(), calls=%async_computation.11 | async-start | bytes 4194304 | tf_op jit(solution)/shard_map/psum | solution.py:187
  82.8 267.2 %copy-start.39 = (f32[1024]{0:T(1024)}, f32[1024]{0:T(1024)S(1)}, u32[]{:S(2)}) copy-start(f32[1024]{0:T(1024)S(1)} %convert_element_type.187) | copy-start | bytes 12292
  146.6 200.9 %copy-start.19 = (bf16[1024,128]{1,0:T(8,128)(2,1)}, bf16[1024,128]{1,0:T(8,128)(2,1)S(1)}, u32[]{:S(2)}) copy-start(bf16[1024,128]{1,0:T(8,128)(2,1)S(1)} %all_gather.27) | copy-start | bytes 786436
  211.4 138.6 %copy-start.21 = (bf16[1024,128]{1,0:T(8,128)(2,1)}, bf16[1024,128]{1,0:T(8,128)(2,1)S(1)}, u32[]{:S(2)}) copy-start(bf16[1024,128]{1,0:T(8,128)(2,1)S(1)} %all_gather.26) | copy-start | bytes 786436
  278.1 70.1 %copy-start.14 = (bf16[1024,256]{1,0:T(8,128)(2,1)}, bf16[1024,256]{1,0:T(8,128)(2,1)S(1)}, u32[]{:S(2)}) copy-start(bf16[1024,256]{1,0:T(8,128)(2,1)S(1)} %all_gather.28) | copy-start | bytes 1572868
  344.0 8.4 copy-start.11
  344.0 3.6 copy-start.9
  345.7 4.4 copy-start.47
  349.5 2.0 copy-start.2
  349.5 2.0 copy-start.43
  350.1 2.2 copy-start.45
  354.7 127.8 %copy-start.35 = (f32[1024]{0:T(1024)}, f32[1024]{0:T(1024)S(1)}, u32[]{:S(2)}) copy-start(f32[1024]{0:T(1024)S(1)} %convert_element_type.199) | copy-start | bytes 12292
  509.0 7.8 copy-start.50
  509.0 166.9 %all-to-all-start = ((bf16[32,160,1024]{2,1,0:T(8,128)(2,1)}), bf16[32,160,1024]{2,1,0:T(8,128)(2,1)}, u32[]{:S(2)}, u32[]{:S(2)}) async-start(bf16[32,160,1024]{2,1,0:T(8,128)(2,1)} %bitcast.227), calls=%async_computation | async-start | bytes 20971520 | tf_op jit(solution)/shard_map/all_to_all | solution.py:123
  516.0 59.1 %all-gather.5.cloned.1.call-start = ((), (), s32[]{:S(2)}) async-start(), calls=%async_computation.13 | async-start | bytes 1310720 | tf_op jit(solution)/shard_map/all_gather | solution.py:211
  675.8 174.1 %all-to-all-start.2 = ((bf16[32,160,1024]{2,1,0:T(8,128)(2,1)}), bf16[32,160,1024]{2,1,0:T(8,128)(2,1)}, u32[]{:S(2)}, u32[]{:S(2)}) async-start(bf16[32,160,1024]{2,1,0:T(8,128)(2,1)} %bitcast.228), calls=%async_computation.3 | async-start | bytes 20971520 | tf_op jit(solution)/shard_map/all_to_all | solution.py:123
  692.8 8.4 copy-start.17
  849.9 10.7 copy-start.18
  860.6 8.7 copy-start.15
  883.5 171.8 %all-to-all-start.3 = ((bf16[32,160,1024]{2,1,0:T(8,128)(2,1)}), bf16[32,160,1024]{2,1,0:T(8,128)(2,1)}, u32[]{:S(2)}, u32[]{:S(2)}) async-start(bf16[32,160,1024]{2,1,0:T(8,128)(2,1)} %add_convert_fusion), calls=%async_computation.4 | async-start | bytes 20971520 | tf_op jit(solution)/shard_map/all_to_all | solution.py:127
  908.9 170.0 %copy-start.38 = (s32[4096,1]{0,1:T(1,128)S(1)}, s32[4096,1]{0,1:T(1,128)}, u32[]{:S(2)}) copy-start(s32[4096,1]{0,1:T(1,128)} %compare_select_fusion) | copy-start | bytes 49156
  1055.3 175.4 %all-to-all-start.1 = ((bf16[32,160,1024]{2,1,0:T(8,128)(2,1)}), bf16[32,160,1024]{2,1,0:T(8,128)(2,1)}, u32[]{:S(2)}, u32[]{:S(2)}) async-start(bf16[32,160,1024]{2,1,0:T(8,128)(2,1)} %convolution_convert_fusion), calls=%async_computation.1 | async-start | bytes 20971520 | tf_op jit(solution)/shard_map/all_to_all | solution.py:127
  1078.9 188.1 %all-reduce.12.cloned.1.call-start = ((), (), s32[]{:S(2)}) async-start(), calls=%async_computation.14 | async-start | bytes 4194304 | tf_op jit(solution)/shard_map/psum | solution.py:245
  1105.5 11.9 copy-start.36
  1105.6 11.9 copy-start.42
  1117.5 2.9 copy-start.8
  1122.1 3.2 copy-start.44
  1122.1 3.2 copy-start.46
  1122.2 291.2 %reduce-scatter.7.cloned.1.call-start = ((), (), s32[]{:S(2)}) async-start(), calls=%async_computation.12 | async-start | bytes 1310720 | tf_op jit(solution)/shard_map/reduce_scatter | solution.py:207
  1230.8 26.5 %copy-start.13 = (f32[512,8]{1,0:T(8,128)S(1)}, f32[512,8]{1,0:T(8,128)}, u32[]{:S(2)}) copy-start(f32[512,8]{1,0:T(8,128)} %copy.54) | copy-start | bytes 49156
  1266.9 186.3 %reduce-scatter.15.cloned.1.call-start = ((), (), s32[]{:S(2)}) async-start(), calls=%async_computation.18 | async-start | bytes 270336 | tf_op jit(solution)/shard_map/reduce_scatter | solution.py:287
  1267.0 2.3 copy-start.12
  1267.0 3.3 copy-start.3
  1273.1 3.5 copy-start.4
  1276.6 2.5 copy-start.23
  1280.7 330.5 %reduce-scatter.13.cloned.1.call-start = ((), (), s32[]{:S(2)}) async-start(), calls=%async_computation.17 | async-start | bytes 270336 | tf_op jit(solution)/shard_map/reduce_scatter | solution.py:284
  1283.2 8.4 copy-start.25
  1283.2 485.8 %reduce-scatter.17.cloned.1.call-start = ((), (), s32[]{:S(2)}) async-start(), calls=%async_computation.19 | async-start | bytes 540672 | tf_op jit(solution)/shard_map/reduce_scatter | solution.py:290
  1283.4 8.2 copy-start.6
  1292.9 635.4 %reduce-scatter.11.cloned.1.call-start = ((), (), s32[]{:S(2)}) async-start(), calls=%async_computation.16 | async-start | bytes 540672 | tf_op jit(solution)/shard_map/reduce_scatter | solution.py:281
  1295.2 2.2 copy-start.29
  1297.5 2.9 copy-start.20
  1300.3 684.2 %reduce-scatter.9.cloned.1.call-start = ((), (), s32[]{:S(2)}) async-start(), calls=%async_computation.15 | async-start | bytes 1310720 | tf_op jit(solution)/shard_map/reduce_scatter | solution.py:272
  1305.7 7.0 copy-start.16
  1312.7 6.5 copy-start.49
  1312.7 673.7 %copy-start.1 = (bf16[1,128,1024]{2,1,0:T(8,128)(2,1)S(1)}, bf16[1,128,1024]{2,1,0:T(8,128)(2,1)}, u32[]{:S(2)}) copy-start(bf16[1,128,1024]{2,1,0:T(8,128)(2,1)} %param.24) | copy-start | bytes 786436
  (18 other events, 23.3 us)
Sparse Core Ops, SparseCore 0:
  9.7 24.6 all-gather.2
  354.3 126.1 all-reduce.9
  518.6 56.4 all-gather.4
  1122.3 124.2 all-reduce.11
  1267.1 50.1 reduce-scatter.6
  1319.6 133.5 reduce-scatter.14
  1455.6 155.5 reduce-scatter.12
  1613.6 155.3 reduce-scatter.16
  1771.9 156.3 reduce-scatter.10
  1931.0 53.4 reduce-scatter.8
where the time goes:
time: 2000 us; the launch traced here: 1990 us
  waiting for transfers between devices  1200 us (60%)
  blocking collectives  421 us (21%)
  matrix products  106 us (5%)
  other arithmetic  91.7 us (5%)
  local copies, waits for them, and re-layouts  91.4 us (5%)
  starting transfers between devices  66.9 us (3%)
    all_to_all x2, waiting for transfers between devices, return_slots(): return lax.all_to_all(slots, 'dp', split_axis=0, concat_axis=0, tiled=True)  251 us
    all_to_all x2, waiting for transfers between devices, send_slots(): return lax.all_to_all(slots, 'dp', split_axis=0, concat_axis=0, tiled=True)  212 us
    reduce_scatter x1, waiting for transfers between devices, on_device(): lax.psum_scatter(grad_wq.astype(jnp.bfloat16), 'dp', scatter_dimension=0,...  158 us
    reduce_scatter x1, waiting for transfers between devices, on_device(): lax.psum_scatter(grad_wk.astype(jnp.bfloat16), 'dp', scatter_dimension=0,...  157 us
    reduce_scatter x1, waiting for transfers between devices, on_device(): lax.psum_scatter(grad_wo.astype(jnp.bfloat16), 'dp', scatter_dimension=0,...  157 us
    unnamed x3, blocking collectives  153 us
    psum x1, waiting for transfers between devices, on_device(): mixed = rows + lax.psum(partial_value, 'tensor')  114 us
    all_gather x1, blocking collectives, on_device(): lax.all_gather(w_out, 'dp', axis=0, tiled=True)  65.9 us
  transfers between devices with their start and end apart: 14, of which 11 were waited for; matrix products, arithmetic and copies ran while one was open for 11% of the time, Pallas kernels for 0%

commit v1 on v0

v1 whole, which is shorter than its diff:
```python
import jax
import jax.numpy as jnp
from jax import lax
from jax.sharding import PartitionSpec as P

HD = 64
DOCS = 3
EPS = 1e-06
THETA = 10000.0
BF = jnp.bfloat16
F32 = jnp.float32


def dot(a, b, dims):
    return lax.dot_general(a, b, (dims, ((), ())), preferred_element_type=F32)


def swap(x, mask):
    count = lax.axis_size("tensor")
    return lax.ppermute(x, "tensor", [(i, i ^ mask) for i in range(count)])


def gather_rel(x):
    far = swap(x, 2)
    near = swap(x, 1)
    far_near = swap(far, 1)
    return [x, near, far, far_near]


def scatter_rel(blocks):
    got = swap(jnp.stack([blocks[1], blocks[3]]).astype(BF), 1)
    mine = blocks[0].astype(F32) + got[0].astype(F32)
    other = (blocks[2].astype(F32) + got[1].astype(F32)).astype(BF)
    return mine + swap(other, 2).astype(F32)


def sum_tensor(x):
    x = x + swap(x, 1)
    return x + swap(x, 2)


def exchange(x):
    return lax.all_to_all(x, "dp", split_axis=0, concat_axis=0, tiled=True)


def gather_dp(x):
    count = lax.axis_size("dp")
    out = exchange(jnp.broadcast_to(x[None], (count,) + x.shape))
    return out.reshape(count * x.shape[0], x.shape[1])


def scatter_dp(x):
    count = lax.axis_size("dp")
    parts = exchange(x.reshape(count, x.shape[0] // count, x.shape[1]))
    return jnp.sum(parts.astype(F32), axis=0)


def rms_forward(rows):
    inverse = lax.rsqrt(jnp.mean(rows * rows, axis=1, keepdims=True) + EPS)
    return (rows * inverse, inverse)


def doc_positions(segment, index):
    onehot = (segment[:, None] == jnp.arange(DOCS, dtype=jnp.int32)[None, :]).astype(jnp.int32)
    counts = jnp.sum(onehot, axis=0)
    starts = jnp.cumsum(counts) - counts
    first = jnp.sum(onehot * starts[None, :], axis=1)
    return index - first


def rotate(values, cosine, sine, heads):
    half = HD // 2
    out = []
    for h in range(heads):
        first = values[:, h * HD : h * HD + half]
        second = values[:, h * HD + half : (h + 1) * HD]
        out.append(first * cosine - second * sine)
        out.append(second * cosine + first * sine)
    return jnp.concatenate(out, axis=1)


def on_device(
    tokens,
    cotangent,
    norm1_gain,
    w_query,
    w_key,
    w_value,
    w_out,
    norm2_gain,
    expert_gate,
    expert_up,
    expert_down,
    route_gates,
    routes,
    segment,
):
    group = segment.shape[0]
    local, width = tokens.shape
    top_k = routes.shape[1]
    dp_count = lax.axis_size("dp")
    tensor_count = lax.axis_size("tensor")
    experts = expert_gate.shape[0] * dp_count
    capacity = min(group, group * top_k * 5 // (4 * experts))
    share = capacity // tensor_count
    slots = experts * share
    piece = width // dp_count
    here = lax.axis_index("tensor")
    scale = HD ** (-0.5)
    qc, kc, vc, oc = w_query.shape[1], w_key.shape[1], w_value.shape[1], w_out.shape[1]
    heads = qc // HD
    kv_heads = kc // HD
    ratio = heads // kv_heads

    qkv_full = gather_dp(jnp.concatenate([w_query, w_key, w_value], axis=1))
    gains = jnp.stack([norm1_gain, norm2_gain], axis=1)
    gains = jnp.pad(gains, ((0, 0), (0, 128 - 2)))
    rest_full = gather_dp(jnp.concatenate([w_out, gains], axis=1))
    wo = rest_full[:, :oc]
    gain1 = rest_full[:, oc].astype(F32)
    gain2 = rest_full[:, oc + 1].astype(F32)

    blocks = jnp.arange(tensor_count, dtype=jnp.int32) ^ here
    index = (blocks[:, None] * local + jnp.arange(local, dtype=jnp.int32)[None, :]).reshape(group)

    def reorder(x):
        split = x.reshape((tensor_count, local) + x.shape[1:])
        return jnp.concatenate(
            [lax.dynamic_index_in_dim(split, here ^ s, 0, False) for s in range(tensor_count)]
        )

    seg = reorder(segment)
    route_rows = reorder(routes)
    gate_rows = reorder(route_gates)
    rows = jnp.concatenate(gather_rel(tokens)).astype(F32)
    cot_rows = jnp.concatenate(gather_rel(cotangent))

    expert_ids = jnp.arange(experts, dtype=jnp.int32)
    hit = route_rows[None, :, :] == expert_ids[:, None, None]
    member = jnp.any(hit, axis=2)
    gate_of = jnp.sum(jnp.where(hit, gate_rows[None], 0.0), axis=2)
    before = (index[:, None] < index[None, :]).astype(BF)
    slot = dot(member.astype(BF), before, ((1,), (0,)))
    slot = jnp.where(member, slot, -1.0).astype(jnp.int32)
    wanted = here * share + jnp.arange(share, dtype=jnp.int32)
    place = slot[:, None, :] == wanted[None, :, None]
    slot_gate = jnp.sum(jnp.where(place, gate_of[:, None, :], 0.0), axis=2).reshape(slots)
    place = place.astype(BF).reshape(slots, group)

    grad_packed = (dot(place, cot_rows, ((1,), (0,))) * slot_gate[:, None]).astype(BF)
    grad_arrived = exchange(grad_packed.reshape(experts, share, width)).reshape(slots, width)

    normal1, inverse1 = rms_forward(rows)
    normed1 = (normal1 * gain1[None, :]).astype(BF)
    places = doc_positions(seg, index).astype(F32)
    freqs = THETA ** (-(jnp.arange(HD // 2, dtype=F32) * 2.0) / HD)
    angle = places[:, None] * freqs[None, :]
    cosine, sine = jnp.cos(angle), jnp.sin(angle)
    projected = dot(normed1, qkv_full, ((1,), (0,)))
    queries = rotate(projected[:, :qc], cosine, sine, heads).astype(BF)
    keys = rotate(projected[:, qc : qc + kc], cosine, sine, kv_heads).astype(BF)
    values = projected[:, qc + kc :].astype(BF)
    queries = queries.reshape(group, kv_heads, ratio, HD)
    keys = keys.reshape(group, kv_heads, HD)
    values = values.reshape(group, kv_heads, HD)
    allowed = (seg[:, None] == seg[None, :]) & (index[None, :] <= index[:, None])
    scores = jnp.einsum("qkrd,skd->krqs", queries, keys, preferred_element_type=F32) * scale
    scores = jnp.where(allowed[None, None], scores, -1e30)
    top = jnp.max(scores, axis=3, keepdims=True)
    weights = jnp.exp(scores - top)
    probs = weights / jnp.sum(weights, axis=3, keepdims=True)
    probs_low = probs.astype(BF)
    attended = jnp.einsum("krqs,skd->qkrd", probs_low, values, preferred_element_type=F32)
    attended = attended.astype(BF).reshape(group, qc)
    partial = dot(attended, wo, ((1,), (1,))).astype(BF).reshape(tensor_count, local, width)
    mixed = tokens.astype(F32) + scatter_rel(partial)

    normal2, inverse2 = rms_forward(mixed)
    normed2 = (normal2 * gain2[None, :]).astype(BF)
    normed2_rows = jnp.concatenate(gather_rel(normed2))
    packed = dot(place, normed2_rows, ((1,), (0,))).astype(BF)
    arrived = exchange(packed.reshape(experts, share, width)).reshape(slots, width)

    wg = jnp.concatenate(gather_rel(expert_gate[0]), axis=1)
    wu = jnp.concatenate(gather_rel(expert_up[0]), axis=1)
    wd = jnp.concatenate(gather_rel(expert_down[0]), axis=0)
    gate_pre = dot(arrived, wg, ((1,), (0,)))
    up_pre = dot(arrived, wu, ((1,), (0,)))
    sigma = jax.nn.sigmoid(gate_pre)
    silu = gate_pre * sigma
    hidden = (silu * up_pre).astype(BF)
    grad_hidden = dot(grad_arrived, wd, ((1,), (1,)))
    grad_gate_pre = (grad_hidden * up_pre * sigma * (1.0 + gate_pre * (1.0 - sigma))).astype(BF)
    grad_up_pre = (grad_hidden * silu).astype(BF)
    grad_inputs = (
        dot(grad_gate_pre, wg, ((1,), (1,))) + dot(grad_up_pre, wu, ((1,), (1,)))
    ).astype(BF)
    grad_back = exchange(grad_inputs.reshape(experts, share, width)).reshape(slots, width)
    produced = dot(hidden, wd, ((1,), (0,))).astype(BF)
    returned = exchange(produced.reshape(experts, share, width)).reshape(slots, width)
    grad_down = dot(hidden, grad_arrived, ((0,), (0,)))
    grad_gate = dot(arrived, grad_gate_pre, ((0,), (0,)))
    grad_up = dot(arrived, grad_up_pre, ((0,), (0,)))
    units = expert_gate.shape[2]
    grad_gate = scatter_rel([grad_gate[:, s * units : (s + 1) * units] for s in range(tensor_count)])
    grad_up = scatter_rel([grad_up[:, s * units : (s + 1) * units] for s in range(tensor_count)])
    grad_down = scatter_rel([grad_down[s * units : (s + 1) * units] for s in range(tensor_count)])

    weighted = (returned.astype(F32) * slot_gate[:, None]).astype(BF)
    moe = dot(place, weighted, ((0,), (0,))).astype(BF)
    output = mixed + scatter_rel(moe.reshape(tensor_count, local, width))

    grad_normed2 = dot(place, grad_back, ((0,), (0,))).astype(BF)
    grad_normed2 = scatter_rel(grad_normed2.reshape(tensor_count, local, width))
    scaled = grad_normed2 * gain2[None, :]
    inner = jnp.mean(scaled * normal2, axis=1, keepdims=True)
    grad_mixed = cotangent.astype(F32) + inverse2 * (scaled - normal2 * inner)
    gain2_part = sum_tensor(jnp.sum(grad_normed2 * normal2, axis=0, keepdims=True))
    grad_branch = jnp.concatenate(gather_rel(grad_mixed.astype(BF)))

    grad_wo = dot(grad_branch, attended, ((0,), (0,)))
    grad_attended = dot(grad_branch, wo, ((1,), (0,))).astype(BF)
    grad_attended = grad_attended.reshape(group, kv_heads, ratio, HD)
    grad_probs = jnp.einsum("qkrd,skd->krqs", grad_attended, values, preferred_element_type=F32)
    inner = jnp.sum(probs * grad_probs, axis=3, keepdims=True)
    grad_scores = (probs * (grad_probs - inner)).astype(BF)
    grad_q = jnp.einsum("krqs,skd->qkrd", grad_scores, keys, preferred_element_type=F32) * scale
    grad_k = jnp.einsum("krqs,qkrd->skd", grad_scores, queries, preferred_element_type=F32) * scale
    grad_v = jnp.einsum("krqs,qkrd->skd", probs_low, grad_attended, preferred_element_type=F32)
    grad_q = rotate(grad_q.reshape(group, qc), cosine, -sine, heads).astype(BF)
    grad_k = rotate(grad_k.reshape(group, kc), cosine, -sine, kv_heads).astype(BF)
    grad_qkv = jnp.concatenate([grad_q, grad_k, grad_v.reshape(group, vc).astype(BF)], axis=1)
    grad_w = dot(normed1, grad_qkv, ((0,), (0,)))
    grad_normed1 = dot(grad_qkv, qkv_full, ((1,), (1,)))
    gain1_part = sum_tensor(jnp.sum(grad_normed1 * normal1, axis=0, keepdims=True))
    grad_normed1 = scatter_rel(grad_normed1.astype(BF).reshape(tensor_count, local, width))
    scaled = grad_normed1 * gain1[None, :]
    inner = jnp.mean(scaled * normal1[:local], axis=1, keepdims=True)
    grad_tokens = grad_mixed + inverse1[:local] * (scaled - normal1[:local] * inner)

    def with_gain(grads, gain_part):
        column = jnp.pad(gain_part.reshape(width, 1), ((0, 0), (0, 127)))
        return jnp.concatenate([grads, column], axis=1).astype(BF)

    wo_sum = scatter_dp(with_gain(grad_wo, gain2_part))
    w_sum = scatter_dp(with_gain(grad_w, gain1_part))
    own = piece // tensor_count
    gain2_grad = lax.dynamic_slice_in_dim(wo_sum[:, oc], here * own, own, 0)
    gain1_grad = lax.dynamic_slice_in_dim(w_sum[:, qc + kc + vc], here * own, own, 0)
    return (
        output,
        grad_tokens,
        gain1_grad,
        w_sum[:, :qc],
        w_sum[:, qc : qc + kc],
        w_sum[:, qc + kc : qc + kc + vc],
        wo_sum[:, :oc],
        gain2_grad,
        grad_gate[None],
        grad_up[None],
        grad_down[None],
    )


def solution(mesh):
    in_specs = (
        P(("dp", "tensor"), None),
        P(("dp", "tensor"), None),
        P("dp"),
        P("dp", "tensor"),
        P("dp", "tensor"),
        P("dp", "tensor"),
        P("dp", "tensor"),
        P("dp"),
        P("dp", None, "tensor"),
        P("dp", None, "tensor"),
        P("dp", "tensor", None),
        P("dp", None),
        P("dp", None),
        P("dp"),
    )
    out_specs = (
        P(("dp", "tensor"), None),
        P(("dp", "tensor"), None),
        P(("dp", "tensor")),
        P("dp", "tensor"),
        P("dp", "tensor"),
        P("dp", "tensor"),
        P("dp", "tensor"),
        P(("dp", "tensor")),
        P("dp", None, "tensor"),
        P("dp", None, "tensor"),
        P("dp", "tensor", None),
    )
    return jax.shard_map(
        on_device, mesh=mesh, in_specs=in_specs, out_specs=out_specs, check_vma=False
    )
```

time: 2000 us -> 400 us (0.20)
  waiting for transfers between devices: 1200 us -> 169 us
  blocking collectives: 421 us -> 0 us
  local copies, waits for them, and re-layouts: 91.4 us -> 13 us
  other arithmetic: 91.7 us -> 39 us
  matrix products: 106 us -> 75.1 us
  starting transfers between devices: 66.9 us -> 95.2 us
    reduce_scatter x6 -> x0, waiting for transfers between devices: 564 us -> none  [the longest x1 158 us: on_device(): lax.psum_scatter(grad_wq.astype(jnp.bfloat16), 'dp', scatter_dimension=0,...]
    all_to_all x4 -> x8, waiting for transfers between devices: 463 us -> 58.5 us  [exchange(): return lax.all_to_all(x, 'dp', split_axis=0, concat_axis=0, tiled=True)]
    all_gather x4 -> x0, blocking collectives: 258 us -> none  [the longest x1 65.9 us: on_device(): lax.all_gather(w_out, 'dp', axis=0, tiled=True)]
    unnamed x3 -> x0, blocking collectives: 153 us -> none
    psum x2 -> x0, waiting for transfers between devices: 114 us -> none  [the longest x1 114 us: on_device(): mixed = rows + lax.psum(partial_value, 'tensor')]
    ppermute x0 -> x39, waiting for transfers between devices: none -> 110 us  [swap(): return lax.ppermute(x, 'tensor', [(i, i ^ mask) for i in range(count)])]
    all_gather x2 -> x0, waiting for transfers between devices: 56.5 us -> none  [the longest x1 56.5 us: on_device(): lax.all_gather(cotangent, 'tensor', axis=0, tiled=True).astype(jnp.float32)]
    gather x2 -> x0, local copies, waits for them, and re-layouts: 53.1 us -> none  [the longest x1 26.6 us: on_device(): grad_back.reshape(experts * capacity, width)[dest]]
  transfers between devices with their start and end apart: 14 -> 47, of which waited for: 11 -> 15; matrix products, arithmetic and copies ran while one was open for 11% -> 27% of each run, Pallas kernels for 0% -> 0%
where the time goes in v1:
time: 400 us; the launch traced here: 393 us
  waiting for transfers between devices  169 us (42%)
  starting transfers between devices  95.2 us (24%)
  matrix products  75.1 us (19%)
  other arithmetic  39 us (10%)
  local copies, waits for them, and re-layouts  13 us (3%)
    ppermute x39, waiting for transfers between devices, swap(): return lax.ppermute(x, 'tensor', [(i, i ^ mask) for i in range(count)])  110 us
    dot_general x20, matrix products, dot(): return lax.dot_general(a, b, (dims, ((), ())), preferred_element_type=F32)  63.1 us
    all_to_all x8, waiting for transfers between devices, exchange(): return lax.all_to_all(x, 'dp', split_axis=0, concat_axis=0, tiled=True)  58.5 us
    ppermute x39, starting transfers between devices, swap(): return lax.ppermute(x, 'tensor', [(i, i ^ mask) for i in range(count)])  49.3 us
    all_to_all x8, starting transfers between devices, exchange(): return lax.all_to_all(x, 'dp', split_axis=0, concat_axis=0, tiled=True)  45.8 us
  transfers between devices with their start and end apart: 47, of which 15 were waited for; matrix products, arithmetic and copies ran while one was open for 27% of the time, Pallas kernels for 0%

profile of v1, /device:TPU:1, one launch (start us, length us, event | category | flops | bytes accessed | tf_op | source)
XLA Modules:
  0.0 393.1 jit_solution(3919642530513303489)
XLA Ops:
  0.7 4.5 %collective-permute-start.1 = (bf16[128,1024]{1,0:T(8,128)(2,1)}, bf16[128,1024]{1,0:T(8,128)(2,1)S(1)}, u32[]{:S(2)}, u32[]{:S(2)}) collective-permute-start(bf16[128,1024]{1,0:T(8,128)(2,1)} %param.14), channel_id=1, source_target_pairs={{0,2},{1,3},{2,0},{3,1},{4,6},{5,7},{6,4},{7,5},{8,10},{9,11},{10,... | collective-permute-start | bytes 786440 | tf_op jit(solution)/shard_map/ppermute | solution.py:20
  8.9 7.9 %all-to-all-start = ((bf16[32,32,384]{2,1,0:T(8,128)(2,1)}), bf16[32,32,384]{2,1,0:T(8,128)(2,1)S(1)}, u32[]{:S(2)}, u32[]{:S(2)}) async-start(bf16[32,32,384]{2,1,0:T(8,128)(2,1)} %broadcast_in_dim.54), calls=%async_computation | async-start | bytes 1572864 | tf_op jit(solution)/shard_map/all_to_all | solution.py:43
  20.7 10.3 %all-to-all-done = bf16[32,32,384]{2,1,0:T(8,128)(2,1)S(1)} async-done(((bf16[32,32,384]{2,1,0:T(8,128)(2,1)}), bf16[32,32,384]{2,1,0:T(8,128)(2,1)S(1)}, u32[]{:S(2)}, u32[]{:S(2)}) %all-to-all-start) | async-done | bytes 786464 | tf_op jit(solution)/shard_map/all_to_all | solution.py:43
  32.4 3.9 all-to-all-start.1
  39.4 4.0 %multiply_convert_fusion = bf16[1280,1024]{1,0:T(8,128)(2,1)} fusion(pred[1280,512]{1,0:T(32,128)(4,1)S(1)} %bitcast_compare_fusion, f32[1280]{0:T(1024)S(1)} %mul.407, bf16[128,1024]{1,0:T(8,128)(2,1)S(1)} %collective-permute-done.21, bf16[128,1024]{1,0:T(8,128)(2,1)} %collective-permute-done.20, bf16[128,1024]{1,0:T(8,128)(2,1)} %collective-permute-done.19, ...), kind=kOutput, calls=%fused_computation.2 | convolution fusion | flops 1348993024 | bytes 4330496 | tf_op jit(solution)/shard_map/dot_general | solution.py:15
  43.8 8.5 %all-to-all-done.1 = bf16[32,32,512]{2,1,0:T(8,128)(2,1)S(1)} async-done(((bf16[32,32,512]{2,1,0:T(8,128)(2,1)}), bf16[32,32,512]{2,1,0:T(8,128)(2,1)S(1)}, u32[]{:S(2)}, u32[]{:S(2)}) %all-to-all-start.1) | async-done | bytes 1048608 | tf_op jit(solution)/shard_map/all_to_all | solution.py:43
  53.3 4.6 %all-to-all-start.4 = ((bf16[32,40,1024]{2,1,0:T(8,128)(2,1)}), bf16[32,40,1024]{2,1,0:T(8,128)(2,1)S(1)}, u32[]{:S(2)}, u32[]{:S(2)}) async-start(bf16[32,40,1024]{2,1,0:T(8,128)(2,1)} %bitcast.284), calls=%async_computation.4 | async-start | bytes 5242880 | tf_op jit(solution)/shard_map/all_to_all | solution.py:43
  64.5 5.3 %fusion.194 = (f32[2,2,512]{2,1,0:T(2,128)}, f32[2,2,512,512]{2,3,1,0:T(8,128)}) fusion(pred[512,512]{0,1:T(8,128)(4,1)} %compare_and_fusion, bf16[512,2,64,1]{0,2,3,1:T(8,128)(2,1)S(1)} %bitcast.298, bf16[512,2,2,64]{0,3,2,1:T(8,128)(2,1)} %bitcast.300), kind=kOutput, calls=%fused_computation.349 | convolution fusion | flops 138412544 | bytes 4857856 | tf_op jit(solution)/shard_map/sub | solution.py:170
  69.8 2.7 convolution_convert_fusion.6
  73.1 2.9 collective-permute-start.3
  77.6 3.4 collective-permute-start.4
  81.0 19.4 %collective-permute-done.4 = bf16[128,1024]{1,0:T(8,128)(2,1)S(1)} collective-permute-done((bf16[128,1024]{1,0:T(8,128)(2,1)S(1)}, bf16[128,1024]{1,0:T(8,128)(2,1)S(1)}, u32[]{:S(2)}, u32[]{:S(2)}) %collective-permute-start.4) | collective-permute-done | bytes 262176 | tf_op jit(solution)/shard_map/ppermute | solution.py:20
  101.4 8.5 %collective-permute-done.6 = bf16[128,1024]{1,0:T(8,128)(2,1)S(1)} collective-permute-done((bf16[128,1024]{1,0:T(8,128)(2,1)S(1)}, bf16[128,1024]{1,0:T(8,128)(2,1)S(1)}, u32[]{:S(2)}, u32[]{:S(2)}) %collective-permute-start.6) | collective-permute-done | bytes 262176 | tf_op jit(solution)/shard_map/ppermute | solution.py:20
  112.3 3.1 convolution_convert_fusion
  115.4 6.3 %all-to-all-start.2 = ((bf16[32,40,1024]{2,1,0:T(8,128)(2,1)}), bf16[32,40,1024]{2,1,0:T(8,128)(2,1)}, u32[]{:S(2)}, u32[]{:S(2)}) async-start(bf16[32,40,1024]{2,1,0:T(8,128)(2,1)} %bitcast.285), calls=%async_computation.2 | async-start | bytes 5242880 | tf_op jit(solution)/shard_map/all_to_all | solution.py:43
  121.8 2.9 collective-permute-start.12
  126.0 31.1 %collective-permute-done.15 = bf16[128,1024]{1,0:T(8,128)(2,1)S(1)} collective-permute-done((bf16[128,1024]{1,0:T(8,128)(2,1)}, bf16[128,1024]{1,0:T(8,128)(2,1)S(1)}, u32[]{:S(2)}, u32[]{:S(2)}) %collective-permute-start.15) | collective-permute-done | bytes 262176 | tf_op jit(solution)/shard_map/ppermute | solution.py:20
  157.6 5.0 %collective-permute-done.12 = bf16[1024,128]{1,0:T(8,128)(2,1)S(1)} collective-permute-done((bf16[1024,128]{1,0:T(8,128)(2,1)S(1)}, bf16[1024,128]{1,0:T(8,128)(2,1)S(1)}, u32[]{:S(2)}, u32[]{:S(2)}) %collective-permute-start.12) | collective-permute-done | bytes 262176 | tf_op jit(solution)/shard_map/ppermute | solution.py:20
  163.3 5.0 %collective-permute-done.9 = bf16[1024,128]{1,0:T(8,128)(2,1)} collective-permute-done((bf16[1024,128]{1,0:T(8,128)(2,1)}, bf16[1024,128]{1,0:T(8,128)(2,1)}, u32[]{:S(2)}, u32[]{:S(2)}) %collective-permute-start.9) | collective-permute-done | bytes 262176 | tf_op jit(solution)/shard_map/ppermute | solution.py:20
  169.0 4.2 %fusion.73 = f32[1280,512]{1,0:T(8,128)} fusion(bf16[1280,1024]{1,0:T(8,128)(2,1)S(1)} %bitcast.270, bf16[128,1024]{1,0:T(8,128)(2,1)S(1)} %collective-permute-done.16, bf16[128,1024]{1,0:T(8,128)(2,1)S(1)} %collective-permute-done.15, bf16[128,1024]{1,0:T(8,128)(2,1)S(1)} %collective-permute-done.14, bf16[128,1024]{1,0:T(8,128)(2,1)} %bitcast.323), kind=kOutput, calls=%fused_computation.170 | convolution fusion | flops 1346371584 | bytes 6291456 | tf_op jit(solution)/shard_map/dot_general | solution.py:15
  173.9 3.6 fusion.75
  177.6 5.8 %multiply_convert_fusion.4 = (bf16[1280,512]{1,0:T(8,128)(2,1)S(1)}, bf16[1280,512]{1,0:T(8,128)(2,1)S(1)}, bf16[1280,512]{1,0:T(8,128)(2,1)}) fusion(f32[1280,512]{1,0:T(8,128)S(1)} %copy-done.63, f32[1280,512]{1,0:T(8,128)S(1)} %fusion.75, bf16[1280,1024]{1,0:T(8,128)(2,1)} %bitcast.33, bf16[1024,128]{1,0:T(8,128)(2,1)} %collective-permute-done.10, ...), kind=kOutput, calls=%fused_computation.25 | convolution fusion | flops 1356201984 | bytes 12845056 | tf_op jit(solution)/shard_map/dot_general | solution.py:15
  183.3 2.7 fusion.74
  186.1 4.1 %add_convert_fusion = bf16[1280,1024]{1,0:T(8,128)(2,1)} fusion(f32[1280,1024]{1,0:T(8,128)S(1)} %fusion.74, bf16[1280,512]{1,0:T(8,128)(2,1)S(1)} %get-tuple-element.19, bf16[1024,128]{1,0:T(8,128)(2,1)} %collective-permute-done.10, bf16[1024,128]{1,0:T(8,128)(2,1)} %collective-permute-done.9, bf16[1024,128]{1,0:T(8,128)(2,1)} %collective-permute-done.8, ...), kind=kOutput, calls=%fused_computation.1 | convolution fusion | flops 1348993024 | bytes 10223616 | tf_op jit(solution)/shard_map/dot_general | solution.py:15
  190.2 6.8 %all-to-all-start.5 = ((bf16[32,40,1024]{2,1,0:T(8,128)(2,1)}), bf16[32,40,1024]{2,1,0:T(8,128)(2,1)}, u32[]{:S(2)}, u32[]{:S(2)}) async-start(bf16[32,40,1024]{2,1,0:T(8,128)(2,1)} %bitcast.286), calls=%async_computation.5 | async-start | bytes 5242880 | tf_op jit(solution)/shard_map/all_to_all | solution.py:43
  197.0 4.3 %fusion.197 = (bf16[512,1024]{1,0:T(8,128)(2,1)S(1)}, f32[512,1024]{1,0:T(8,128)}) fusion(bf16[1280,512]{1,0:T(8,128)(2,1)} %get-tuple-element.21, bf16[1280,1024]{1,0:T(8,128)(2,1)S(1)} %bitcast.271), kind=kOutput, calls=%fused_computation.352 | convolution fusion | flops 1342701568 | bytes 7077888 | tf_op jit(solution)/shard_map/dot_general | solution.py:15
  202.8 3.1 convolution_convert_fusion.1
  205.9 4.9 %fusion.196 = (bf16[1024,512]{1,0:T(8,128)(2,1)}, f32[1024,512]{1,0:T(8,128)}) fusion(bf16[1280,1024]{1,0:T(8,128)(2,1)} %bitcast.33, bf16[1280,512]{1,0:T(8,128)(2,1)S(1)} %copy-done.62), kind=kOutput, calls=%fused_computation.351 | convolution fusion | flops 1342701568 | bytes 7077888 | tf_op jit(solution)/shard_map/dot_general | solution.py:15
  210.8 24.9 %all-to-all-done.5 = bf16[32,40,1024]{2,1,0:T(8,128)(2,1)} async-done(((bf16[32,40,1024]{2,1,0:T(8,128)(2,1)}), bf16[32,40,1024]{2,1,0:T(8,128)(2,1)}, u32[]{:S(2)}, u32[]{:S(2)}) %all-to-all-start.5) | async-done | bytes 2621472 | tf_op jit(solution)/shard_map/all_to_all | solution.py:43
  235.7 5.1 %all-to-all-start.3 = ((bf16[32,40,1024]{2,1,0:T(8,128)(2,1)}), bf16[32,40,1024]{2,1,0:T(8,128)(2,1)}, u32[]{:S(2)}, u32[]{:S(2)}) async-start(bf16[32,40,1024]{2,1,0:T(8,128)(2,1)} %bitcast.37), calls=%async_computation.3 | async-start | bytes 5242880 | tf_op jit(solution)/shard_map/all_to_all | solution.py:43
  240.9 4.7 %fusion.195 = (bf16[1024,512]{1,0:T(8,128)(2,1)S(1)}, f32[1024,512]{1,0:T(8,128)}) fusion(bf16[1280,1024]{1,0:T(8,128)(2,1)} %bitcast.33, bf16[1280,512]{1,0:T(8,128)(2,1)S(1)} %copy-done.60), kind=kOutput, calls=%fused_computation.350 | convolution fusion | flops 1342701568 | bytes 7077888 | tf_op jit(solution)/shard_map/dot_general | solution.py:15
  250.2 4.2 %collective-permute-start.38 = (bf16[128,1024]{1,0:T(8,128)(2,1)}, bf16[128,1024]{1,0:T(8,128)(2,1)}, u32[]{:S(2)}, u32[]{:S(2)}) collective-permute-start(bf16[128,1024]{1,0:T(8,128)(2,1)} %fusion.44), channel_id=1, source_target_pairs={{0,2},{1,3},{2,0},{3,1},{4,6},{5,7},{6,4},{7,5},{8,10},{9,11},{10,... | collective-permute-start | bytes 786440 | tf_op jit(solution)/shard_map/ppermute | solution.py:20
  254.5 3.4 bitcast_convert_fusion
  260.5 14.8 %all-to-all-done.3 = bf16[32,40,1024]{2,1,0:T(8,128)(2,1)} async-done(((bf16[32,40,1024]{2,1,0:T(8,128)(2,1)}), bf16[32,40,1024]{2,1,0:T(8,128)(2,1)}, u32[]{:S(2)}, u32[]{:S(2)}) %all-to-all-start.3) | async-done | bytes 2621472 | tf_op jit(solution)/shard_map/all_to_all | solution.py:43
  275.3 3.6 bitcast_convert_fusion.1
  282.5 4.3 %collective-permute-start.36 = (bf16[1024,128]{1,0:T(8,128)(2,1)S(1)}, bf16[1024,128]{1,0:T(8,128)(2,1)S(1)}, u32[]{:S(2)}, u32[]{:S(2)}) collective-permute-start(bf16[1024,128]{1,0:T(8,128)(2,1)S(1)} %fusion.47), channel_id=1, source_target_pairs={{0,2},{1,3},{2,0},{3,1},{4,6},{5,7},{6,4},{7,5},{8,10},{9,11},{10,... | collective-permute-start | bytes 786440 | tf_op jit(solution)/shard_map/ppermute | solution.py:20
  288.8 2.9 collective-permute-start.34
  291.9 7.0 %collective-permute-done.23 = bf16[128,1024]{1,0:T(8,128)(2,1)S(1)} collective-permute-done((bf16[128,1024]{1,0:T(8,128)(2,1)S(1)}, bf16[128,1024]{1,0:T(8,128)(2,1)S(1)}, u32[]{:S(2)}, u32[]{:S(2)}) %collective-permute-start.23) | collective-permute-done | bytes 262176 | tf_op jit(solution)/shard_map/ppermute | solution.py:20
  299.2 10.9 %collective-permute-done.18 = bf16[128,1024]{1,0:T(8,128)(2,1)S(1)} collective-permute-done((bf16[128,1024]{1,0:T(8,128)(2,1)S(1)}, bf16[128,1024]{1,0:T(8,128)(2,1)S(1)}, u32[]{:S(2)}, u32[]{:S(2)}) %collective-permute-start.18) | collective-permute-done | bytes 262176 | tf_op jit(solution)/shard_map/ppermute | solution.py:20
  311.6 2.7 collective-permute-start.25
  317.5 3.0 collective-permute-done.25
  335.4 4.1 %all-to-all-start.7 = ((bf16[32,32,384]{2,1,0:T(8,128)(2,1)}), bf16[32,32,384]{2,1,0:T(8,128)(2,1)S(1)}, u32[]{:S(2)}, u32[]{:S(2)}) async-start(bf16[32,32,384]{2,1,0:T(8,128)(2,1)} %pad_maximum_fusion.6), calls=%async_computation.7 | async-start | bytes 1572864 | tf_op jit(solution)/shard_map/all_to_all | solution.py:43
  343.4 3.3 multiply_reduce_fusion
  348.1 3.0 collective-permute-start.30
  351.0 3.0 convolution_convert_fusion.3
  354.3 2.4 pad_maximum_fusion
  356.7 7.2 %all-to-all-start.6 = ((bf16[32,32,640]{2,1,0:T(8,128)(2,1)}), bf16[32,32,640]{2,1,0:T(8,128)(2,1)S(1)}, u32[]{:S(2)}, u32[]{:S(2)}) async-start(bf16[32,32,640]{2,1,0:T(8,128)(2,1)} %pad_maximum_fusion), calls=%async_computation.6 | async-start | bytes 2621440 | tf_op jit(solution)/shard_map/all_to_all | solution.py:43
  370.2 17.3 %collective-permute-done.28 = bf16[128,1024]{1,0:T(8,128)(2,1)S(1)} collective-permute-done((bf16[128,1024]{1,0:T(8,128)(2,1)S(1)}, bf16[128,1024]{1,0:T(8,128)(2,1)S(1)}, u32[]{:S(2)}, u32[]{:S(2)}) %collective-permute-start.28) | collective-permute-done | bytes 262176 | tf_op jit(solution)/shard_map/ppermute | solution.py:20
  (313 shorter events, 80.3 us)
Async XLA Ops:
  0.7 18.9 %collective-permute-start.1 = (bf16[128,1024]{1,0:T(8,128)(2,1)}, bf16[128,1024]{1,0:T(8,128)(2,1)S(1)}, u32[]{:S(2)}, u32[]{:S(2)}) collective-permute-start(bf16[128,1024]{1,0:T(8,128)(2,1)} %param.14), channel_id=1, source_target_pairs={{0,2},{1,3},{2,0},{3,1},{4,6},{5,7},{6,4},{7,5},{8,10},{9,11},{10,... | collective-permute-start | bytes 786440 | tf_op jit(solution)/shard_map/ppermute | solution.py:20
  5.2 32.8 %collective-permute-start = (bf16[128,1024]{1,0:T(8,128)(2,1)}, bf16[128,1024]{1,0:T(8,128)(2,1)}, u32[]{:S(2)}, u32[]{:S(2)}) collective-permute-start(bf16[128,1024]{1,0:T(8,128)(2,1)} %param.14), channel_id=1, source_target_pairs={{0,1},{1,0},{2,3},{3,2},{4,5},{5,4},{6,7},{7,6},{8,9},{9,8},{10,11... | collective-permute-start | bytes 786440 | tf_op jit(solution)/shard_map/ppermute | solution.py:20
  6.2 30.2 %collective-permute-start.20 = (bf16[128,1024]{1,0:T(8,128)(2,1)}, bf16[128,1024]{1,0:T(8,128)(2,1)}, u32[]{:S(2)}, u32[]{:S(2)}) collective-permute-start(bf16[128,1024]{1,0:T(8,128)(2,1)} %param.15), channel_id=1, source_target_pairs={{0,2},{1,3},{2,0},{3,1},{4,6},{5,7},{6,4},{7,5},{8,10},{9,11},{10,... | collective-permute-start | bytes 786440 | tf_op jit(solution)/shard_map/ppermute | solution.py:20
  6.2 33.2 %collective-permute-start.19 = (bf16[128,1024]{1,0:T(8,128)(2,1)}, bf16[128,1024]{1,0:T(8,128)(2,1)}, u32[]{:S(2)}, u32[]{:S(2)}) collective-permute-start(bf16[128,1024]{1,0:T(8,128)(2,1)} %param.15), channel_id=1, source_target_pairs={{0,1},{1,0},{2,3},{3,2},{4,5},{5,4},{6,7},{7,6},{8,9},{9,8},{10,11... | collective-permute-start | bytes 786440 | tf_op jit(solution)/shard_map/ppermute | solution.py:20
  8.9 22.2 %all-to-all-start = ((bf16[32,32,384]{2,1,0:T(8,128)(2,1)}), bf16[32,32,384]{2,1,0:T(8,128)(2,1)S(1)}, u32[]{:S(2)}, u32[]{:S(2)}) async-start(bf16[32,32,384]{2,1,0:T(8,128)(2,1)} %broadcast_in_dim.54), calls=%async_computation | async-start | bytes 1572864 | tf_op jit(solution)/shard_map/all_to_all | solution.py:43
  19.6 18.5 %collective-permute-start.2 = (bf16[128,1024]{1,0:T(8,128)(2,1)S(1)}, bf16[128,1024]{1,0:T(8,128)(2,1)}, u32[]{:S(2)}, u32[]{:S(2)}) collective-permute-start(bf16[128,1024]{1,0:T(8,128)(2,1)S(1)} %collective-permute-done.1), channel_id=1, source_target_pairs={{0,1},{1,0},{2,3},{3,2},{4,5},{5,4},{6,7},{7,6},{8,9},{9,8},{10,11... | collective-permute-start | bytes 786440 | tf_op jit(solution)/shard_map/ppermute | solution.py:20
  31.1 41.4 %copy-start.1 = (bf16[32,32,384]{2,1,0:T(8,128)(2,1)}, bf16[32,32,384]{2,1,0:T(8,128)(2,1)S(1)}, u32[]{:S(2)}) copy-start(bf16[32,32,384]{2,1,0:T(8,128)(2,1)S(1)} %all-to-all-done) | copy-start | bytes 2359300
  32.4 19.9 %all-to-all-start.1 = ((bf16[32,32,512]{2,1,0:T(8,128)(2,1)}), bf16[32,32,512]{2,1,0:T(8,128)(2,1)S(1)}, u32[]{:S(2)}, u32[]{:S(2)}) async-start(bf16[32,32,512]{2,1,0:T(8,128)(2,1)} %broadcast_in_dim.55), calls=%async_computation.1 | async-start | bytes 2097152 | tf_op jit(solution)/shard_map/all_to_all | solution.py:43
  36.4 3.1 collective-permute-start.21
  53.3 62.1 %all-to-all-start.4 = ((bf16[32,40,1024]{2,1,0:T(8,128)(2,1)}), bf16[32,40,1024]{2,1,0:T(8,128)(2,1)S(1)}, u32[]{:S(2)}, u32[]{:S(2)}) async-start(bf16[32,40,1024]{2,1,0:T(8,128)(2,1)} %bitcast.284), calls=%async_computation.4 | async-start | bytes 5242880 | tf_op jit(solution)/shard_map/all_to_all | solution.py:43
  73.1 4.4 %collective-permute-start.3 = (bf16[2,128,1024]{2,1,0:T(8,128)(2,1)S(1)}, bf16[2,128,1024]{2,1,0:T(8,128)(2,1)S(1)}, u32[]{:S(2)}, u32[]{:S(2)}) collective-permute-start(bf16[2,128,1024]{2,1,0:T(8,128)(2,1)S(1)} %pad_maximum_fusion.7), channel_id=1, source_target_pairs={{0,1},{1,0},{2,3},{3,2},{4,5},{5,4},{6,7},{7,6},{8,9},{9,8},{10,11... | collective-permute-start | bytes 1572872 | tf_op jit(solution)/shard_map/ppermute | solution.py:20
  77.6 22.8 %collective-permute-start.4 = (bf16[128,1024]{1,0:T(8,128)(2,1)S(1)}, bf16[128,1024]{1,0:T(8,128)(2,1)S(1)}, u32[]{:S(2)}, u32[]{:S(2)}) collective-permute-start(bf16[128,1024]{1,0:T(8,128)(2,1)S(1)} %fusion.61), channel_id=1, source_target_pairs={{0,2},{1,3},{2,0},{3,1},{4,6},{5,7},{6,4},{7,5},{8,10},{9,11},{10,... | collective-permute-start | bytes 786440 | tf_op jit(solution)/shard_map/ppermute | solution.py:20
  100.8 9.1 %collective-permute-start.6 = (bf16[128,1024]{1,0:T(8,128)(2,1)S(1)}, bf16[128,1024]{1,0:T(8,128)(2,1)S(1)}, u32[]{:S(2)}, u32[]{:S(2)}) collective-permute-start(bf16[128,1024]{1,0:T(8,128)(2,1)S(1)} %multiply_convert_fusion.9), channel_id=1, source_target_pairs={{0,2},{1,3},{2,0},{3,1},{4,6},{5,7},{6,4},{7,5},{8,10},{9,11},{10,... | collective-permute-start | bytes 786440 | tf_op jit(solution)/shard_map/ppermute | solution.py:20
  100.9 10.2 %collective-permute-start.5 = (bf16[128,1024]{1,0:T(8,128)(2,1)S(1)}, bf16[128,1024]{1,0:T(8,128)(2,1)S(1)}, u32[]{:S(2)}, u32[]{:S(2)}) collective-permute-start(bf16[128,1024]{1,0:T(8,128)(2,1)S(1)} %multiply_convert_fusion.9), channel_id=1, source_target_pairs={{0,1},{1,0},{2,3},{3,2},{4,5},{5,4},{6,7},{7,6},{8,9},{9,8},{10,11... | collective-permute-start | bytes 786440 | tf_op jit(solution)/shard_map/ppermute | solution.py:20
  109.9 2.4 collective-permute-start.7
  115.4 58.5 %all-to-all-start.2 = ((bf16[32,40,1024]{2,1,0:T(8,128)(2,1)}), bf16[32,40,1024]{2,1,0:T(8,128)(2,1)}, u32[]{:S(2)}, u32[]{:S(2)}) async-start(bf16[32,40,1024]{2,1,0:T(8,128)(2,1)} %bitcast.285), calls=%async_computation.2 | async-start | bytes 5242880 | tf_op jit(solution)/shard_map/all_to_all | solution.py:43
  121.7 35.4 %collective-permute-start.15 = (bf16[128,1024]{1,0:T(8,128)(2,1)}, bf16[128,1024]{1,0:T(8,128)(2,1)S(1)}, u32[]{:S(2)}, u32[]{:S(2)}) collective-permute-start(bf16[128,1024]{1,0:T(8,128)(2,1)} %bitcast.321), channel_id=1, source_target_pairs={{0,2},{1,3},{2,0},{3,1},{4,6},{5,7},{6,4},{7,5},{8,10},{9,11},{10,... | collective-permute-start | bytes 786440 | tf_op jit(solution)/shard_map/ppermute | solution.py:20
  121.8 40.8 %collective-permute-start.12 = (bf16[1024,128]{1,0:T(8,128)(2,1)S(1)}, bf16[1024,128]{1,0:T(8,128)(2,1)S(1)}, u32[]{:S(2)}, u32[]{:S(2)}) collective-permute-start(bf16[1024,128]{1,0:T(8,128)(2,1)S(1)} %bitcast.313), channel_id=1, source_target_pairs={{0,2},{1,3},{2,0},{3,1},{4,6},{5,7},{6,4},{7,5},{8,10},{9,11},{10,... | collective-permute-start | bytes 786440 | tf_op jit(solution)/shard_map/ppermute | solution.py:20
  124.8 38.4 %collective-permute-start.14 = (bf16[128,1024]{1,0:T(8,128)(2,1)}, bf16[128,1024]{1,0:T(8,128)(2,1)S(1)}, u32[]{:S(2)}, u32[]{:S(2)}) collective-permute-start(bf16[128,1024]{1,0:T(8,128)(2,1)} %bitcast.322), channel_id=1, source_target_pairs={{0,1},{1,0},{2,3},{3,2},{4,5},{5,4},{6,7},{7,6},{8,9},{9,8},{10,11... | collective-permute-start | bytes 786440 | tf_op jit(solution)/shard_map/ppermute | solution.py:20
  126.0 42.4 %collective-permute-start.9 = (bf16[1024,128]{1,0:T(8,128)(2,1)}, bf16[1024,128]{1,0:T(8,128)(2,1)}, u32[]{:S(2)}, u32[]{:S(2)}) collective-permute-start(bf16[1024,128]{1,0:T(8,128)(2,1)} %bitcast.317), channel_id=1, source_target_pairs={{0,2},{1,3},{2,0},{3,1},{4,6},{5,7},{6,4},{7,5},{8,10},{9,11},{10,... | collective-permute-start | bytes 786440 | tf_op jit(solution)/shard_map/ppermute | solution.py:20
  157.1 11.9 %collective-permute-start.16 = (bf16[128,1024]{1,0:T(8,128)(2,1)S(1)}, bf16[128,1024]{1,0:T(8,128)(2,1)S(1)}, u32[]{:S(2)}, u32[]{:S(2)}) collective-permute-start(bf16[128,1024]{1,0:T(8,128)(2,1)S(1)} %collective-permute-done.15), channel_id=1, source_target_pairs={{0,1},{1,0},{2,3},{3,2},{4,5},{5,4},{6,7},{7,6},{8,9},{9,8},{10,11... | collective-permute-start | bytes 786440 | tf_op jit(solution)/shard_map/ppermute | solution.py:20
  157.6 15.6 %collective-permute-start.11 = (bf16[1024,128]{1,0:T(8,128)(2,1)S(1)}, bf16[1024,128]{1,0:T(8,128)(2,1)S(1)}, u32[]{:S(2)}, u32[]{:S(2)}) collective-permute-start(bf16[1024,128]{1,0:T(8,128)(2,1)S(1)} %bitcast.314), channel_id=1, source_target_pairs={{0,1},{1,0},{2,3},{3,2},{4,5},{5,4},{6,7},{7,6},{8,9},{9,8},{10,11... | collective-permute-start | bytes 786440 | tf_op jit(solution)/shard_map/ppermute | solution.py:20
  162.6 14.9 %collective-permute-start.8 = (bf16[1024,128]{1,0:T(8,128)(2,1)}, bf16[1024,128]{1,0:T(8,128)(2,1)}, u32[]{:S(2)}, u32[]{:S(2)}) collective-permute-start(bf16[1024,128]{1,0:T(8,128)(2,1)} %bitcast.318), channel_id=1, source_target_pairs={{0,1},{1,0},{2,3},{3,2},{4,5},{5,4},{6,7},{7,6},{8,9},{9,8},{10,11... | collective-permute-start | bytes 786440 | tf_op jit(solution)/shard_map/ppermute | solution.py:20
  163.2 10.7 %collective-permute-start.13 = (bf16[1024,128]{1,0:T(8,128)(2,1)S(1)}, bf16[1024,128]{1,0:T(8,128)(2,1)}, u32[]{:S(2)}, u32[]{:S(2)}) collective-permute-start(bf16[1024,128]{1,0:T(8,128)(2,1)S(1)} %collective-permute-done.12), channel_id=1, source_target_pairs={{0,1},{1,0},{2,3},{3,2},{4,5},{5,4},{6,7},{7,6},{8,9},{9,8},{10,11... | collective-permute-start | bytes 786440 | tf_op jit(solution)/shard_map/ppermute | solution.py:20
  168.3 9.2 %collective-permute-start.10 = (bf16[1024,128]{1,0:T(8,128)(2,1)}, bf16[1024,128]{1,0:T(8,128)(2,1)}, u32[]{:S(2)}, u32[]{:S(2)}) collective-permute-start(bf16[1024,128]{1,0:T(8,128)(2,1)} %collective-permute-done.9), channel_id=1, source_target_pairs={{0,1},{1,0},{2,3},{3,2},{4,5},{5,4},{6,7},{7,6},{8,9},{9,8},{10,11... | collective-permute-start | bytes 786440 | tf_op jit(solution)/shard_map/ppermute | solution.py:20
  190.2 45.5 %all-to-all-start.5 = ((bf16[32,40,1024]{2,1,0:T(8,128)(2,1)}), bf16[32,40,1024]{2,1,0:T(8,128)(2,1)}, u32[]{:S(2)}, u32[]{:S(2)}) async-start(bf16[32,40,1024]{2,1,0:T(8,128)(2,1)} %bitcast.286), calls=%async_computation.5 | async-start | bytes 5242880 | tf_op jit(solution)/shard_map/all_to_all | solution.py:43
  201.4 47.1 %collective-permute-start.37 = (bf16[2,128,1024]{2,1,0:T(8,128)(2,1)S(1)}, bf16[2,128,1024]{2,1,0:T(8,128)(2,1)}, u32[]{:S(2)}, u32[]{:S(2)}) collective-permute-start(bf16[2,128,1024]{2,1,0:T(8,128)(2,1)S(1)} %pad_maximum_fusion.13), channel_id=1, source_target_pairs={{0,1},{1,0},{2,3},{3,2},{4,5},{5,4},{6,7},{7,6},{8,9},{9,8},{10,11... | collective-permute-start | bytes 1572872 | tf_op jit(solution)/shard_map/ppermute | solution.py:20
  235.7 39.6 %all-to-all-start.3 = ((bf16[32,40,1024]{2,1,0:T(8,128)(2,1)}), bf16[32,40,1024]{2,1,0:T(8,128)(2,1)}, u32[]{:S(2)}, u32[]{:S(2)}) async-start(bf16[32,40,1024]{2,1,0:T(8,128)(2,1)} %bitcast.37), calls=%async_computation.3 | async-start | bytes 5242880 | tf_op jit(solution)/shard_map/all_to_all | solution.py:43
  246.5 34.9 %collective-permute-start.35 = (bf16[2,1024,128]{2,1,0:T(8,128)(2,1)}, bf16[2,1024,128]{2,1,0:T(8,128)(2,1)}, u32[]{:S(2)}, u32[]{:S(2)}) collective-permute-start(bf16[2,1024,128]{2,1,0:T(8,128)(2,1)} %pad_maximum_fusion.12), channel_id=1, source_target_pairs={{0,1},{1,0},{2,3},{3,2},{4,5},{5,4},{6,7},{7,6},{8,9},{9,8},{10,11... | collective-permute-start | bytes 1572872 | tf_op jit(solution)/shard_map/ppermute | solution.py:20
  248.5 38.4 %collective-permute-start.33 = (bf16[2,1024,128]{2,1,0:T(8,128)(2,1)}, bf16[2,1024,128]{2,1,0:T(8,128)(2,1)}, u32[]{:S(2)}, u32[]{:S(2)}) collective-permute-start(bf16[2,1024,128]{2,1,0:T(8,128)(2,1)} %pad_maximum_fusion.11), channel_id=1, source_target_pairs={{0,1},{1,0},{2,3},{3,2},{4,5},{5,4},{6,7},{7,6},{8,9},{9,8},{10,11... | collective-permute-start | bytes 1572872 | tf_op jit(solution)/shard_map/ppermute | solution.py:20
  250.2 65.3 %collective-permute-start.38 = (bf16[128,1024]{1,0:T(8,128)(2,1)}, bf16[128,1024]{1,0:T(8,128)(2,1)}, u32[]{:S(2)}, u32[]{:S(2)}) collective-permute-start(bf16[128,1024]{1,0:T(8,128)(2,1)} %fusion.44), channel_id=1, source_target_pairs={{0,2},{1,3},{2,0},{3,1},{4,6},{5,7},{6,4},{7,5},{8,10},{9,11},{10,... | collective-permute-start | bytes 786440 | tf_op jit(solution)/shard_map/ppermute | solution.py:20
  259.7 27.0 %collective-permute-start.22 = (bf16[2,128,1024]{2,1,0:T(8,128)(2,1)}, bf16[2,128,1024]{2,1,0:T(8,128)(2,1)S(1)}, u32[]{:S(2)}, u32[]{:S(2)}) collective-permute-start(bf16[2,128,1024]{2,1,0:T(8,128)(2,1)} %pad_maximum_fusion.9), channel_id=1, source_target_pairs={{0,1},{1,0},{2,3},{3,2},{4,5},{5,4},{6,7},{7,6},{8,9},{9,8},{10,11... | collective-permute-start | bytes 1572872 | tf_op jit(solution)/shard_map/ppermute | solution.py:20
  279.0 12.7 %collective-permute-start.17 = (bf16[2,128,1024]{2,1,0:T(8,128)(2,1)S(1)}, bf16[2,128,1024]{2,1,0:T(8,128)(2,1)S(1)}, u32[]{:S(2)}, u32[]{:S(2)}) collective-permute-start(bf16[2,128,1024]{2,1,0:T(8,128)(2,1)S(1)} %pad_maximum_fusion.8), channel_id=1, source_target_pairs={{0,1},{1,0},{2,3},{3,2},{4,5},{5,4},{6,7},{7,6},{8,9},{9,8},{10,11... | collective-permute-start | bytes 1572872 | tf_op jit(solution)/shard_map/ppermute | solution.py:20
  282.5 39.9 %collective-permute-start.36 = (bf16[1024,128]{1,0:T(8,128)(2,1)S(1)}, bf16[1024,128]{1,0:T(8,128)(2,1)S(1)}, u32[]{:S(2)}, u32[]{:S(2)}) collective-permute-start(bf16[1024,128]{1,0:T(8,128)(2,1)S(1)} %fusion.47), channel_id=1, source_target_pairs={{0,2},{1,3},{2,0},{3,1},{4,6},{5,7},{6,4},{7,5},{8,10},{9,11},{10,... | collective-permute-start | bytes 786440 | tf_op jit(solution)/shard_map/ppermute | solution.py:20
  286.8 12.1 %collective-permute-start.23 = (bf16[128,1024]{1,0:T(8,128)(2,1)S(1)}, bf16[128,1024]{1,0:T(8,128)(2,1)S(1)}, u32[]{:S(2)}, u32[]{:S(2)}) collective-permute-start(bf16[128,1024]{1,0:T(8,128)(2,1)S(1)} %fusion.56), channel_id=1, source_target_pairs={{0,2},{1,3},{2,0},{3,1},{4,6},{5,7},{6,4},{7,5},{8,10},{9,11},{10,... | collective-permute-start | bytes 786440 | tf_op jit(solution)/shard_map/ppermute | solution.py:20
  288.8 78.0 %collective-permute-start.34 = (bf16[1024,128]{1,0:T(8,128)(2,1)}, bf16[1024,128]{1,0:T(8,128)(2,1)}, u32[]{:S(2)}, u32[]{:S(2)}) collective-permute-start(bf16[1024,128]{1,0:T(8,128)(2,1)} %fusion.50), channel_id=1, source_target_pairs={{0,2},{1,3},{2,0},{3,1},{4,6},{5,7},{6,4},{7,5},{8,10},{9,11},{10,... | collective-permute-start | bytes 786440 | tf_op jit(solution)/shard_map/ppermute | solution.py:20
  291.8 18.3 %collective-permute-start.18 = (bf16[128,1024]{1,0:T(8,128)(2,1)S(1)}, bf16[128,1024]{1,0:T(8,128)(2,1)S(1)}, u32[]{:S(2)}, u32[]{:S(2)}) collective-permute-start(bf16[128,1024]{1,0:T(8,128)(2,1)S(1)} %fusion.58), channel_id=1, source_target_pairs={{0,2},{1,3},{2,0},{3,1},{4,6},{5,7},{6,4},{7,5},{8,10},{9,11},{10,... | collective-permute-start | bytes 786440 | tf_op jit(solution)/shard_map/ppermute | solution.py:20
  311.6 9.0 %collective-permute-start.25 = (bf16[128,1024]{1,0:T(8,128)(2,1)}, bf16[128,1024]{1,0:T(8,128)(2,1)}, u32[]{:S(2)}, u32[]{:S(2)}) collective-permute-start(bf16[128,1024]{1,0:T(8,128)(2,1)} %get-tuple-element.15), channel_id=1, source_target_pairs={{0,2},{1,3},{2,0},{3,1},{4,6},{5,7},{6,4},{7,5},{8,10},{9,11},{10,... | collective-permute-start | bytes 786440 | tf_op jit(solution)/shard_map/ppermute | solution.py:20
  314.3 3.1 collective-permute-start.31
  317.4 7.1 %collective-permute-start.24 = (bf16[128,1024]{1,0:T(8,128)(2,1)}, bf16[128,1024]{1,0:T(8,128)(2,1)S(1)}, u32[]{:S(2)}, u32[]{:S(2)}) collective-permute-start(bf16[128,1024]{1,0:T(8,128)(2,1)} %get-tuple-element.15), channel_id=1, source_target_pairs={{0,1},{1,0},{2,3},{3,2},{4,5},{5,4},{6,7},{7,6},{8,9},{9,8},{10,11... | collective-permute-start | bytes 786440 | tf_op jit(solution)/shard_map/ppermute | solution.py:20
  317.4 6.8 %collective-permute-start.32 = (f32[1,1024]{1,0:T(1,128)S(1)}, f32[1,1024]{1,0:T(1,128)S(1)}, u32[]{:S(2)}, u32[]{:S(2)}) collective-permute-start(f32[1,1024]{1,0:T(1,128)S(1)} %add.278), channel_id=1, source_target_pairs={{0,2},{1,3},{2,0},{3,1},{4,6},{5,7},{6,4},{7,5},{8,10},{9,11},{10,... | collective-permute-start | bytes 12296 | tf_op jit(solution)/shard_map/ppermute | solution.py:20
  320.5 4.0 %collective-permute-start.26 = (bf16[128,1024]{1,0:T(8,128)(2,1)}, bf16[128,1024]{1,0:T(8,128)(2,1)S(1)}, u32[]{:S(2)}, u32[]{:S(2)}) collective-permute-start(bf16[128,1024]{1,0:T(8,128)(2,1)} %collective-permute-done.25), channel_id=1, source_target_pairs={{0,1},{1,0},{2,3},{3,2},{4,5},{5,4},{6,7},{7,6},{8,9},{9,8},{10,11... | collective-permute-start | bytes 786440 | tf_op jit(solution)/shard_map/ppermute | solution.py:20
  335.4 21.3 %all-to-all-start.7 = ((bf16[32,32,384]{2,1,0:T(8,128)(2,1)}), bf16[32,32,384]{2,1,0:T(8,128)(2,1)S(1)}, u32[]{:S(2)}, u32[]{:S(2)}) async-start(bf16[32,32,384]{2,1,0:T(8,128)(2,1)} %pad_maximum_fusion.6), calls=%async_computation.7 | async-start | bytes 1572864 | tf_op jit(solution)/shard_map/all_to_all | solution.py:43
  346.7 1.4 collective-permute-start.29
  347.6 16.4 %collective-permute-start.27 = (bf16[2,128,1024]{2,1,0:T(8,128)(2,1)}, bf16[2,128,1024]{2,1,0:T(8,128)(2,1)}, u32[]{:S(2)}, u32[]{:S(2)}) collective-permute-start(bf16[2,128,1024]{2,1,0:T(8,128)(2,1)} %pad_maximum_fusion.10), channel_id=1, source_target_pairs={{0,1},{1,0},{2,3},{3,2},{4,5},{5,4},{6,7},{7,6},{8,9},{9,8},{10,11... | collective-permute-start | bytes 1572872 | tf_op jit(solution)/shard_map/ppermute | solution.py:20
  348.1 6.0 %collective-permute-start.30 = (f32[1,1024]{1,0:T(1,128)S(1)}, f32[1,1024]{1,0:T(1,128)S(1)}, u32[]{:S(2)}, u32[]{:S(2)}) collective-permute-start(f32[1,1024]{1,0:T(1,128)S(1)} %add.275), channel_id=1, source_target_pairs={{0,2},{1,3},{2,0},{3,1},{4,6},{5,7},{6,4},{7,5},{8,10},{9,11},{10,... | collective-permute-start | bytes 12296 | tf_op jit(solution)/shard_map/ppermute | solution.py:20
  356.7 33.9 %all-to-all-start.6 = ((bf16[32,32,640]{2,1,0:T(8,128)(2,1)}), bf16[32,32,640]{2,1,0:T(8,128)(2,1)S(1)}, u32[]{:S(2)}, u32[]{:S(2)}) async-start(bf16[32,32,640]{2,1,0:T(8,128)(2,1)} %pad_maximum_fusion), calls=%async_computation.6 | async-start | bytes 2621440 | tf_op jit(solution)/shard_map/all_to_all | solution.py:43
  365.1 22.4 %collective-permute-start.28 = (bf16[128,1024]{1,0:T(8,128)(2,1)S(1)}, bf16[128,1024]{1,0:T(8,128)(2,1)S(1)}, u32[]{:S(2)}, u32[]{:S(2)}) collective-permute-start(bf16[128,1024]{1,0:T(8,128)(2,1)S(1)} %fusion.53), channel_id=1, source_target_pairs={{0,2},{1,3},{2,0},{3,1},{4,6},{5,7},{6,4},{7,5},{8,10},{9,11},{10,... | collective-permute-start | bytes 786440 | tf_op jit(solution)/shard_map/ppermute | solution.py:20
  (64 other events, 646.1 us)
